TPU v7x, 512 devices: a whole 4x4x16 slice. The times are simulated.
512 devices in a mesh: lat: 128 (over y, z, x_hi), lon: 4 (over x_lo, core).
Axes of the slice: x: 4 (x_hi: 2, x_lo: 2; x = x_hi * 2 + x_lo), y: 4, z: 16, core: 2. Of those that a mesh axis runs over, the one named last changes fastest.
Arguments:
- fields: bfloat16 [2, 768, 48, 512], P(None, 'lat', 'lon'), may hold values from -24 to 24
- cotangent: bfloat16 [2, 768, 48, 512], P(None, 'lat', 'lon'), may hold values from -6 to 6
- norm_gain: float32 [512], replicated, may hold values from 0.1 to 1.9
- inner_weight: bfloat16 [512, 1536], replicated, may hold values from -0.25 to 0.25
- outer_weight: bfloat16 [512, 512], replicated, may hold values from -0.25 to 0.25
- bias_table: float32 [8, 759], replicated, may hold values from -4 to 256
- merge_gain: float32 [2048], replicated, may hold values from 0.1 to 1.9
- merge_weight: bfloat16 [2048, 1024], P('lat'), may hold values from -0.125 to 0.125
- split_weight: bfloat16 [1024, 2048], P('lat'), may hold values from -0.1875 to 0.1875
Outputs:
- outputs: bfloat16 [2, 768, 48, 512], P(None, 'lat', 'lon')
- grad_fields: bfloat16 [2, 768, 48, 512], P(None, 'lat', 'lon')
- grad_inner: float32 [512, 1536], P('lat', 'lon')
All inputs are finite; a program needn't handle non-finite values.
Results may differ from a plain program's by a relative error of at most 0.0096.
Values may be sent and summed in bfloat16 or wider, within the bound.
A program may use at most 64 MiB of HBM per device.

v0:
```python
import math

import jax
import jax.numpy as jnp
from jax import lax
from jax.sharding import PartitionSpec as P

D = 512
HEADS = 8
HEAD_DIM = 64
LEVELS = 2
WIN_LAT = 6
WIN_LON = 12
WIN = 144


def passed_along(value, axis, by):
    peers = lax.axis_size(axis)
    return lax.ppermute(value, axis, [(i, (i + by) % peers) for i in range(peers)])


def layer_norm(values, gain_vec):
    mean_of = jnp.mean(values, axis=-1, keepdims=True)
    centred = values - mean_of
    variance = jnp.mean(centred * centred, axis=-1, keepdims=True)
    return centred * lax.rsqrt(variance + 1e-05) * gain_vec


def relative_index():
    position = jnp.arange(WIN, dtype=jnp.int32)
    level_of = position // (WIN_LAT * WIN_LON)
    row_of = position // WIN_LON % WIN_LAT
    column = position % WIN_LON
    level_gap = level_of[:, None] - level_of[None, :] + LEVELS - 1
    row_gap = row_of[:, None] - row_of[None, :] + WIN_LAT - 1
    column_gap = column[:, None] - column[None, :] + WIN_LON - 1
    return (level_gap * (2 * WIN_LAT - 1) + row_gap) * (2 * WIN_LON - 1) + column_gap


def window_allowed(count_lat, count_lon, at_end):
    position = jnp.arange(WIN, dtype=jnp.int32)
    upper_half = position // WIN_LON % WIN_LAT >= WIN_LAT // 2
    window_row = jnp.arange(count_lat * count_lon, dtype=jnp.int32) // count_lon
    last_band = jnp.logical_and(window_row == count_lat - 1, at_end)
    group_of = jnp.logical_and(last_band[:, None], upper_half[None, :])
    return group_of[:, :, None] == group_of[:, None, :]


def to_windows(grid_in):
    levels, row_count, col_count, channels = grid_in.shape
    blocks = grid_in.reshape(
        levels, row_count // WIN_LAT, WIN_LAT, col_count // WIN_LON, WIN_LON, channels
    )
    return blocks.transpose(1, 3, 0, 2, 4, 5).reshape(-1, WIN, channels)


def from_windows(blocks, row_count, col_count):
    channels = blocks.shape[-1]
    grid_in = blocks.reshape(
        row_count // WIN_LAT, col_count // WIN_LON, LEVELS, WIN_LAT, WIN_LON, channels
    )
    return grid_in.transpose(2, 0, 3, 1, 4, 5).reshape(LEVELS, row_count, col_count, channels)


def to_pairs(grid_in):
    levels, row_count, col_count, channels = grid_in.shape
    blocks = grid_in.reshape(levels, row_count // 2, 2, col_count // 2, 2, channels)
    return blocks.transpose(0, 1, 3, 2, 4, 5).reshape(
        levels, row_count // 2, col_count // 2, 4 * channels
    )


def from_pairs(paired, channels):
    levels, half_rows, half_cols = (paired.shape[0], paired.shape[1], paired.shape[2])
    blocks = paired.reshape(levels, half_rows, half_cols, 2, 2, channels)
    return blocks.transpose(0, 1, 3, 2, 4, 5).reshape(
        levels, 2 * half_rows, 2 * half_cols, channels
    )


def roll_in(grid_in):
    half_lat = WIN_LAT // 2
    half_lon = WIN_LON // 2
    border = passed_along(grid_in[:, :, :half_lon], "lon", -1)
    grid_in = jnp.concatenate([grid_in[:, :, half_lon:], border], axis=2)
    border = passed_along(grid_in[:, :half_lat], "lat", -1)
    return jnp.concatenate([grid_in[:, half_lat:], border], axis=1)


def roll_out(grid_in):
    half_lat = WIN_LAT // 2
    half_lon = WIN_LON // 2
    border = passed_along(grid_in[:, -half_lat:], "lat", 1)
    grid_in = jnp.concatenate([border, grid_in[:, :-half_lat]], axis=1)
    border = passed_along(grid_in[:, :, -half_lon:], "lon", 1)
    return jnp.concatenate([border, grid_in[:, :, :-half_lon]], axis=2)


def attend(projected, pos_bias, allowed):
    blocks = projected.shape[0]
    heads = projected.reshape(blocks, WIN, 3, HEADS, HEAD_DIM)
    inv_root = HEAD_DIM ** (-0.5)
    scores = jnp.einsum(
        "bqhe,bkhe->bhqk", heads[:, :, 0], heads[:, :, 1], preferred_element_type=jnp.float32
    )
    scores = scores * inv_root + pos_bias[None]
    scores = jnp.where(allowed[:, None], scores, -1e30)
    attention = jax.nn.softmax(scores, axis=-1)
    attention_b = attention.astype(jnp.bfloat16)
    attended = jnp.einsum(
        "bhqk,bkhe->bqhe", attention_b, heads[:, :, 2], preferred_element_type=jnp.float32
    )
    return (attended.astype(jnp.bfloat16).reshape(blocks, WIN, D), attention, attention_b)


def attend_back(projected, attention, attention_b, grad_attended):
    blocks = projected.shape[0]
    heads = projected.reshape(blocks, WIN, 3, HEADS, HEAD_DIM)
    inv_root = HEAD_DIM ** (-0.5)
    grad_heads = grad_attended.reshape(blocks, WIN, HEADS, HEAD_DIM)
    grad_probs = jnp.einsum(
        "bqhe,bkhe->bhqk", grad_heads, heads[:, :, 2], preferred_element_type=jnp.float32
    )
    grad_values = jnp.einsum(
        "bhqk,bqhe->bkhe", attention_b, grad_heads, preferred_element_type=jnp.float32
    ).astype(jnp.bfloat16)
    grad_scores = attention * (grad_probs - jnp.sum(attention * grad_probs, axis=-1, keepdims=True))
    grad_scores_b = grad_scores.astype(jnp.bfloat16)
    grad_query = (
        jnp.einsum(
            "bhqk,bkhe->bqhe", grad_scores_b, heads[:, :, 1], preferred_element_type=jnp.float32
        )
        * inv_root
    ).astype(jnp.bfloat16)
    grad_keys = (
        jnp.einsum(
            "bhqk,bqhe->bkhe", grad_scores_b, heads[:, :, 0], preferred_element_type=jnp.float32
        )
        * inv_root
    ).astype(jnp.bfloat16)
    return jnp.stack([grad_query, grad_keys, grad_values], axis=2).reshape(blocks, WIN, 3 * D)


def local(
    fields,
    cotangent,
    norm_gain,
    inner_weight,
    outer_weight,
    bias_table,
    merge_gain,
    merge_weight,
    split_weight,
):
    lat_rows = fields.shape[1]
    lon_cols = fields.shape[2]
    contract_last = (((1,), (1,)), ((), ()))
    rolled = roll_in(fields)
    flat_rolled = rolled.reshape(-1, D).astype(jnp.float32)
    normed = layer_norm(flat_rolled, norm_gain).astype(jnp.bfloat16)
    projected = jnp.dot(normed, inner_weight, preferred_element_type=jnp.float32).astype(
        jnp.bfloat16
    )
    windows = to_windows(projected.reshape(LEVELS, lat_rows, lon_cols, 3 * D))
    at_end = lax.axis_index("lat") == lax.axis_size("lat") - 1
    allowed = window_allowed(lat_rows // WIN_LAT, lon_cols // WIN_LON, at_end)
    pos_bias = jnp.take(bias_table, relative_index(), axis=1)
    attended, attention, attention_b = attend(windows, pos_bias, allowed)
    attended = from_windows(attended, lat_rows, lon_cols).reshape(-1, D)
    projected_out = jnp.dot(attended, outer_weight, preferred_element_type=jnp.float32)
    y_rolled = (flat_rolled + projected_out).astype(jnp.bfloat16).reshape(fields.shape)
    y_grid = roll_out(y_rolled)
    full_merge, full_split = (
        lax.all_gather(merge_weight, "lat", axis=0, tiled=True),
        lax.all_gather(split_weight, "lat", axis=0, tiled=True),
    )
    paired = to_pairs(y_grid)
    pair_shape = paired.shape
    pair_flat = paired.reshape(-1, 4 * D).astype(jnp.float32)
    merged_norm = layer_norm(pair_flat, merge_gain).astype(jnp.bfloat16)
    merged = jnp.dot(merged_norm, full_merge, preferred_element_type=jnp.float32).astype(
        jnp.bfloat16
    )
    split_out = jnp.dot(merged, full_split, preferred_element_type=jnp.float32)
    outputs = from_pairs((pair_flat + split_out).astype(jnp.bfloat16).reshape(pair_shape), D)
    grad_paired = to_pairs(cotangent).reshape(-1, 4 * D)
    grad_merged = lax.dot_general(
        grad_paired, full_split, contract_last, preferred_element_type=jnp.float32
    ).astype(jnp.bfloat16)
    grad_mnorm = lax.dot_general(
        grad_merged, full_merge, contract_last, preferred_element_type=jnp.float32
    )
    _, merge_back = jax.vjp(lambda inputs: layer_norm(inputs, merge_gain), pair_flat)
    grad_y_pairs = (grad_paired.astype(jnp.float32) + merge_back(grad_mnorm)[0]).astype(
        jnp.bfloat16
    )
    grad_y = from_pairs(grad_y_pairs.reshape(pair_shape), D)
    grad_rolled_y = roll_in(grad_y)
    flat_grad = grad_rolled_y.reshape(-1, D)
    grad_attended = lax.dot_general(
        flat_grad, outer_weight, contract_last, preferred_element_type=jnp.float32
    ).astype(jnp.bfloat16)
    grad_windows = to_windows(grad_attended.reshape(LEVELS, lat_rows, lon_cols, D))
    grad_projected = attend_back(windows, attention, attention_b, grad_windows)
    grad_projected = from_windows(grad_projected, lat_rows, lon_cols).reshape(-1, 3 * D)
    grad_normed = lax.dot_general(
        grad_projected, inner_weight, contract_last, preferred_element_type=jnp.float32
    )
    _, norm_back = jax.vjp(lambda inputs: layer_norm(inputs, norm_gain), flat_rolled)
    grad_rolled = (flat_grad.astype(jnp.float32) + norm_back(grad_normed)[0]).astype(jnp.bfloat16)
    grad_fields = roll_out(grad_rolled.reshape(fields.shape))
    row_share = lax.psum_scatter(
        lax.dot_general(
            normed, grad_projected, (((0,), (0,)), ((), ())), preferred_element_type=jnp.float32
        ),
        "lat",
        scatter_dimension=0,
        tiled=True,
    )
    grad_share = lax.psum_scatter(row_share, "lon", scatter_dimension=1, tiled=True)
    total_tokens = LEVELS * lat_rows * lax.axis_size("lat") * lon_cols * lax.axis_size("lon")
    grad_inner = grad_share * (1.0 / math.sqrt(total_tokens))
    return (outputs, grad_fields, grad_inner)


def solution(mesh):
    return jax.shard_map(
        local,
        mesh=mesh,
        in_specs=(
            P(None, "lat", "lon", None),
            P(None, "lat", "lon", None),
            P(),
            P(),
            P(),
            P(),
            P(),
            P("lat", None),
            P("lat", None),
        ),
        out_specs=(P(None, "lat", "lon", None), P(None, "lat", "lon", None), P("lat", "lon")),
        check_vma=False,
    )
```

profile of v0, /device:TPU:1, one launch (start us, length us, event | category | flops | bytes accessed | tf_op | source)
XLA Modules:
  0.0 1909.4 jit_solution(2279519010336690227)
XLA Ops:
  9.8 8.8 collective-permute-start
  19.9 12.6 collective-permute-start.1
  33.4 38.7 %gather_fusion = f32[20736,8]{1,0:T(8,128)} fusion(f32[8,759]{0,1:T(8,128)S(1)} %copy.59, s32[21504]{0:T(1024)S(1)} %pad_clamp_fusion), kind=kCustom, calls=%fused_computation | custom fusion | bytes 1410048 | tf_op jit(solution)/shard_map/jit(_take)/gather | solution.py:167
  72.1 11.2 copy.61
  88.2 2.2 copy.86
  90.4 1.5 fusion.4
  93.2 2.2 convolution_convert_fusion.2
  95.8 1.9 collective-permute-start.2
  97.7 10.2 collective-permute-done.2
  108.0 2.6 collective-permute-start.3
  115.5 117.7 %all-gather.5.cloned.1.call-done = bf16[1024,2048]{1,0:T(8,128)(2,1)} async-done(((bf16[8,2048]{1,0:T(8,128)(2,1)}), bf16[1024,2048]{1,0:T(8,128)(2,1)}) %all-gather.5.cloned.1.call-update) | async-done | bytes 4194320 | tf_op jit(solution)/shard_map/all_gather | solution.py:175
  233.2 223.1 %all-gather.3.cloned.1.call-done = bf16[2048,1024]{1,0:T(8,128)(2,1)} async-done(((bf16[16,1024]{1,0:T(8,128)(2,1)}), bf16[2048,1024]{1,0:T(8,128)(2,1)}) %all-gather.3.cloned.1.call-update) | async-done | bytes 4194320 | tf_op jit(solution)/shard_map/all_gather | solution.py:174
  456.3 6.9 multiply_reduce_fusion.1
  465.0 11.1 collective-permute-start.4
  476.1 2.2 collective-permute-done.4
  478.5 7.6 collective-permute-start.5
  488.8 2.9 fusion.8
  495.5 2.3 fusion.44
  501.1 2.3 collective-permute-start.6
  503.5 5.1 fusion.1
  509.5 3.8 collective-permute-done.6
  513.3 2.6 collective-permute-start.7
  515.9 1273.1 %all-reduce.3.cloned.1.call-done = f32[512,1536]{1,0:T(8,128)} async-done(((f32[512,1536]{1,0:T(8,128)}), f32[512,1536]{1,0:T(8,128)}) %all-reduce.3.cloned.1.call-update) | async-done | bytes 3145744
  1792.0 109.3 %reduce-scatter.4.cloned.1.call-done = f32[384,4]{1,0:T(8,128)} async-done(((f32[1536,4]{1,0:T(8,128)}), f32[384,4]{1,0:T(8,128)}) %reduce-scatter.4.cloned.1.call-update) | async-done | bytes 6160
  (140 shorter events, 32.3 us)
Async XLA Ops:
  7.2 79.8 %copy-start = (bf16[512,1536]{1,0:T(8,128)(2,1)S(1)}, bf16[512,1536]{1,0:T(8,128)(2,1)}, u32[]{:S(2)}) copy-start(bf16[512,1536]{1,0:T(8,128)(2,1)} %param.12) | copy-start | bytes 4718596
  7.2 26.0 %copy-start.13 = (f32[8,759]{1,0:T(8,128)S(1)}, f32[8,759]{1,0:T(8,128)}, u32[]{:S(2)}) copy-start(f32[8,759]{1,0:T(8,128)} %param.14) | copy-start | bytes 72868
  7.2 226.0 %all-gather.5.cloned.1.call-start = ((), (), s32[]{:S(2)}) async-start(), calls=%async_computation.2 | async-start | bytes 4227072 | tf_op jit(solution)/shard_map/all_gather | solution.py:175
  7.9 448.4 %all-gather.3.cloned.1.call-start = ((), (), s32[]{:S(2)}) async-start(), calls=%async_computation.1 | async-start | bytes 4227072 | tf_op jit(solution)/shard_map/all_gather | solution.py:174
  8.7 1780.3 %all-reduce.3.cloned.1.call-start = ((), (), s32[]{:S(2)}) async-start(), calls=%async_computation.4 | async-start | bytes 6291456
  9.8 9.9 collective-permute-start
  19.9 63.4 %collective-permute-start.1 = (bf16[2,3,12,512]{3,0,2,1:T(2,128)(2,1)S(1)}, bf16[2,3,12,512]{3,0,2,1:T(2,128)(2,1)S(1)}, u32[]{:S(2)}, u32[]{:S(2)}) collective-permute-start(bf16[2,3,12,512]{3,0,2,1:T(2,128)(2,1)S(1)} %get-tuple-element.22), channel_id=1, source_target_pairs={{0,508},{4,0},{8,4},{12,8},{16,12},{20,16},{24,20},{28,24},{32,28}... | collective-permute-start | bytes 221192 | tf_op jit(solution)/shard_map/ppermute | solution.py:19
  84.0 3.0 copy-start.14
  86.8 3.5 copy-start.17
  86.8 3.5 copy-start.15
  95.4 15.1 copy-start.9
  95.8 12.2 collective-permute-start.2
  108.0 4.2 collective-permute-start.3
  112.3 344.1 %copy-start.12 = (f32[2048]{0:T(1024)S(1)}, f32[2048]{0:T(1024)}, u32[]{:S(2)}) copy-start(f32[2048]{0:T(1024)} %param.15) | copy-start | bytes 24580
  115.0 348.3 %copy-start.19 = (f32[36]{0:T(128)}, f32[36]{0:T(128)S(1)}, u32[]{:S(2)}) copy-start(f32[36]{0:T(128)S(1)} %div.108) | copy-start | bytes 436
  464.5 21.6 %copy-start.6 = (bf16[2,3,12,512]{3,0,2,1:T(2,128)(2,1)S(1)}, bf16[2,3,12,512]{3,0,2,1:T(2,128)(2,1)}, u32[]{:S(2)}) copy-start(bf16[2,3,12,512]{3,0,2,1:T(2,128)(2,1)} %copy-done.5) | copy-start | bytes 221188
  465.0 13.3 collective-permute-start.4
  478.5 8.8 collective-permute-start.5
  488.8 2.9 copy-start.1
  497.9 1403.3 %reduce-scatter.4.cloned.1.call-start = ((), (), s32[]{:S(2)}) async-start(), calls=%async_computation.3 | async-start | bytes 983040
  500.7 2.8 copy-start.20
  500.7 2.8 copy-start.22
  501.1 12.1 collective-permute-start.6
  513.3 1277.8 %collective-permute-start.7 = (bf16[2,6,6,512]{3,2,1,0:T(8,128)(2,1)S(1)}, bf16[2,6,6,512]{3,2,1,0:T(8,128)(2,1)S(1)}, u32[]{:S(2)}, u32[]{:S(2)}) collective-permute-start(bf16[2,6,6,512]{3,2,1,0:T(8,128)(2,1)S(1)} %fusion.27), channel_id=1, source_target_pairs={{0,1},{1,2},{2,3},{3,0},{4,5},{5,6},{6,7},{7,4},{8,9},{9,10},{10,1... | collective-permute-start | bytes 221192 | tf_op jit(solution)/shard_map/ppermute | solution.py:19
  (11 other events, 15.0 us)
Sparse Core Ops, SparseCore 0:
  12.5 220.6 all-gather.4
  237.7 218.6 all-gather.2
  498.0 1290.9 all-reduce.2
  1792.0 109.2 reduce-scatter.3
where the time goes:
time: 1910 us
  waiting for transfers between devices  1740 us (91%)
  local copies, waits for them, and re-layouts  66.9 us (4%)
  starting transfers between devices  49.7 us (3%)
  matrix products  25.4 us (1%)
    unnamed x6, waiting for transfers between devices  1380 us
    all_gather x1, waiting for transfers between devices, local(): lax.all_gather(merge_weight, 'lat', axis=0, tiled=True)  223 us
    all_gather x1, waiting for transfers between devices, local(): lax.all_gather(split_weight, 'lat', axis=0, tiled=True)  118 us
    gather x2, local copies, waits for them, and re-layouts, local(): pos_bias = jnp.take(bias_table, relative_index(), axis=1)  49.9 us
    ppermute x8, starting transfers between devices, passed_along(): lax.ppermute(value, axis, [(i, (i + by) % peers) for i in range(peers)])  49.6 us
  transfers between devices with their start and end apart: 12, of which 9 were waited for; matrix products, arithmetic and copies ran while one was open for 4% of the time, Pallas kernels for 0%

commit v1 on v0

v1 whole, which is shorter than its diff:
```python
import functools
import math

import jax
import jax.numpy as jnp
import ml_dtypes
import numpy as np
from jax import lax
from jax.experimental import pallas as pl
from jax.experimental.pallas import tpu as pltpu
from jax.sharding import PartitionSpec as P

LEVELS = 2
WIN_LAT = 6
WIN_LON = 12
HEADS = 8
RELS = 759
SPAN = 384
QUAD = 48
ROWS = 4 * QUAD
WIN = 144
FAR = -1e30
Y, Z, XH = 4, 16, 2
MESH = pl.DeviceIdType.MESH
NT = (((1,), (1,)), ((), ()))
TN = (((0,), (0,)), ((), ()))
F32 = jnp.float32
BF16 = jnp.bfloat16


def dot(a, b, dims=(((1,), (0,)), ((), ()))):
    return lax.dot_general(a, b, dims, preferred_element_type=F32)


def orders():
    natural, quarter, pair = {}, {}, {}
    base, compact = {}, {}
    for l in range(LEVELS):
        for r in range(WIN_LAT):
            for c in range(WIN_LON):
                token = (l, r, c)
                natural[token] = (l * WIN_LAT + r) * 16 + c
                inside = (l * 3 + r % 3) * 6 + c % 6
                quarter[token] = ((r // 3) * 2 + c // 6) * QUAD + inside
                compact[token] = ((r // 3) * 2 + c // 6) * 36 + inside
                pair[token] = ((r % 2) * 2 + c % 2) * QUAD + (l * 3 + r // 2) * 6 + c // 2
                base[token] = (l * (2 * WIN_LAT - 1) + r) * (2 * WIN_LON - 1) + c
    to_quarter = np.zeros((ROWS, ROWS), ml_dtypes.bfloat16)
    to_pair = np.zeros((ROWS, ROWS), ml_dtypes.bfloat16)
    pair_of_quarter = np.zeros((ROWS, ROWS), ml_dtypes.bfloat16)
    dense = np.zeros((WIN, ROWS), ml_dtypes.bfloat16)
    pick = np.zeros((ROWS, SPAN), ml_dtypes.bfloat16)
    for token in natural:
        to_quarter[quarter[token], natural[token]] = 1
        to_pair[pair[token], natural[token]] = 1
        pair_of_quarter[pair[token], quarter[token]] = 1
        dense[compact[token], quarter[token]] = 1
        pick[quarter[token], base[token]] = 1
    return to_quarter, to_pair, pair_of_quarter, dense, pick


def bias_kernel(wrapped_ref, pick_ref, bias_ref):
    pick = pick_ref[...]
    used = jnp.sum(dot(jnp.ones((8, SPAN), BF16), pick, NT), axis=0, keepdims=True) > 0.5
    for h in range(HEADS):
        row = jnp.broadcast_to(wrapped_ref[h : h + 1, :], (SPAN, 2 * SPAN))
        shifted = pltpu.roll(row, 0, 1, stride=1, stride_axis=0)[:, :SPAN]
        high = shifted.astype(BF16)
        rest = shifted - high.astype(F32)
        middle = rest.astype(BF16)
        low = (rest - middle.astype(F32)).astype(BF16)
        total = jnp.zeros((ROWS, ROWS), F32)
        for part in (low, middle, high):
            total = total + dot(dot(pick, part).astype(BF16), pick, NT)
        bias_ref[h] = jnp.where(used, total, FAR)


def norm_parts(values):
    mean = jnp.mean(values, axis=-1, keepdims=True)
    centred = values - mean
    variance = jnp.mean(centred * centred, axis=-1, keepdims=True)
    scale = lax.rsqrt(variance + 1e-05)
    return centred * scale, scale


def norm_back(unit, scale, grad, gain):
    g = grad * gain
    middle = jnp.mean(g, axis=-1, keepdims=True)
    along = jnp.mean(g * unit, axis=-1, keepdims=True)
    return scale * (g - middle - unit * along)


def main_kernel(
    lon_size,
    fields, cotangent, gain, inner, outer, bias, merge_gain, merge_shard, split_shard,
    to_quarter, to_pair, pair_of_quarter, dense,
    outputs, grad_fields, grad_inner,
    nat, quads, win, cot_all, norm_all, raw, stack, split_w, merge_w,
    y_out, y_in, gm_out, gm_in, gy_out, gy_in, gf_out, gf_in, att, proj, normed,
    toks_all, gp, gp_out, gp_in, dw_out, dw_in, z_out, z_in, so_out, so_in, unit_keep,
    ssem, rsem, zsend, zrecv,
):
    D = fields.shape[-1]
    MS = D // 2
    CW = 3 * D // lon_size
    KB = 8
    HD2 = 2 * D // HEADS
    i, j = lax.axis_index("lat"), lax.axis_index("lon")
    lat_size = Y * Z * XH
    xh = lax.rem(i, XH)
    z = lax.rem(i // XH, Z)
    y = i // (XH * Z)

    def at(yy, zz, xx):
        return (yy * Z + zz) * XH + xx

    def lat_by(d):
        return lax.rem(i + d + lat_size, lat_size)

    def lon_by(d):
        return lax.rem(j + d + lon_size, lon_size)

    def y_by(d):
        return lax.rem(y + d + Y, Y)

    def z_by(d):
        return lax.rem(z + d, Z)

    sems = iter(range(ssem.shape[0]))
    sent = []

    def push(src, dst, lat, lon):
        k = next(sems)
        copy = pltpu.make_async_remote_copy(
            src_ref=src, dst_ref=dst, send_sem=ssem.at[k], recv_sem=rsem.at[k],
            device_id=(lat, lon), device_id_type=MESH,
        )
        copy.start()
        sent.append(copy)
        return copy

    def arrive(copies):
        for copy in copies:
            copy.wait_recv()

    def to_natural(src):
        nat[...] = jnp.zeros((ROWS, D), BF16)
        for l in range(LEVELS):
            for r in range(WIN_LAT):
                start = (l * WIN_LAT + r) * 16
                nat[start : start + WIN_LON, :] = src[l, r]
        return nat[...]

    quads[...] = dot(to_quarter[...], to_natural(fields)).astype(BF16).reshape(4, QUAD, D)
    win[0] = quads[3]

    for k in range(KB):
        stack[8 * k : 8 * k + 8, :] = split_shard[:, MS * k : MS * (k + 1)].astype(F32)
    row = lax.broadcasted_iota(jnp.int32, (16, 64), 0)
    col = lax.broadcasted_iota(jnp.int32, (16, 64), 1)
    sel = (col == (row // 2) * 8 + 2 * j + row % 2).astype(F32).astype(BF16)
    raw[z] = dot(sel, stack[...].astype(BF16)).astype(BF16)
    own = lax.broadcasted_iota(jnp.int32, (2 * D, MS), 1)
    place = ((own // (2 * Z * XH)) * Z + (own // 2) % Z) * XH + (own // (2 * Z)) % XH
    col = lax.broadcasted_iota(jnp.int32, (2 * D, MS), 0)
    sel = (col == 8 * place + 2 * j + own % 2).astype(F32).astype(BF16)
    merge_w[y, z, xh] = dot(merge_shard[...], sel).astype(BF16)

    partners = []
    for a, b in ((0, 1), (1, 0), (1, 1)):
        partners += [(lat_by(a), lon_by(b)), (lat_by(-a), lon_by(-b))]
    for d in range(1, lon_size):
        partners.append((i, lon_by(d)))
    plane = [(dy, dx) for dy in range(Y) for dx in range(XH) if dy or dx]
    for dy, dx in plane:
        partners.append((at(y_by(dy), z, lax.rem(xh + dx, XH)), j))
    barrier = pltpu.get_barrier_semaphore()
    for lat, lon in partners:
        pl.semaphore_signal(barrier, inc=1, device_id=(lat, lon), device_id_type=MESH)

    @pl.loop(1, Z)
    def _(d):
        pl.semaphore_signal(
            barrier, inc=1, device_id=(at(y, z_by(d), xh), j), device_id_type=MESH
        )

    pl.semaphore_wait(barrier, len(partners) + Z - 1)

    def roll_in(src, dst):
        return [
            push(src.at[(1 - a) * 2 + 1 - b], dst.at[a * 2 + b], lat_by(-a), lon_by(-b))
            for a, b in ((0, 1), (1, 0), (1, 1))
        ]

    def roll_out(src, dst):
        return [
            push(src.at[a * 2 + b], dst.at[(1 - a) * 2 + 1 - b], lat_by(a), lon_by(b))
            for a, b in ((0, 1), (1, 0), (1, 1))
        ]

    def z_copy(kind, d, src, dst):
        return pltpu.make_async_remote_copy(
            src_ref=src, dst_ref=dst, send_sem=zsend.at[kind, d], recv_sem=zrecv.at[kind, d],
            device_id=(at(y, z_by(d), xh), j), device_id_type=MESH,
        )

    def split_z(d):
        return z_copy(0, d, raw.at[z], raw.at[z])

    def merge_z(d):
        return z_copy(1, d, merge_w.at[y, z, xh], merge_w.at[y, z, xh])

    def sums_z(d):
        return z_copy(2, d, z_out.at[z_by(d)], z_in.at[z])

    def z_start(make):
        @pl.loop(1, Z)
        def _(d):
            make(d).start()

    def z_arrive(make):
        @pl.loop(1, Z)
        def _(d):
            make(d).wait_recv()

    fields_move = roll_in(quads, win)
    z_start(split_z)
    z_start(merge_z)

    def lanes(rows):
        return jnp.concatenate([rows[QUAD * s : QUAD * (s + 1)] for s in range(4)], axis=1)

    def stacked(wide):
        return jnp.concatenate([wide[:, D * s : D * (s + 1)] for s in range(4)], axis=0)

    cot_all[j] = lanes(dot(to_pair[...], to_natural(cotangent)).astype(BF16))
    cot_move = [push(cot_all.at[j], cot_all.at[j], i, lon_by(d)) for d in range(1, lon_size)]

    arrive(fields_move)
    rolled = win[...].reshape(ROWS, D).astype(F32)
    unit, scale = norm_parts(rolled)
    unit_keep[...] = unit
    normed[...] = (unit * gain[...]).astype(BF16)
    proj[...] = dot(normed[...], inner[...]).astype(BF16)

    z_arrive(split_z)
    full = Z * 16
    out = lax.broadcasted_iota(jnp.int32, (full, full), 0)
    src = lax.broadcasted_iota(jnp.int32, (full, full), 1)
    want = ((out % (2 * Z)) // 2) * 16 + (out // (2 * Z)) * 2 + out % 2
    regroup = (src == want).astype(F32).astype(BF16)
    split_w[y, xh] = dot(regroup, raw[...].reshape(full, MS)).astype(BF16).reshape(KB, 2 * Z, MS)
    other = lax.rem(xh + 1, XH)
    split_x = push(split_w.at[y, xh], split_w.at[y, xh], at(y, z, other), j)

    half_q = lax.broadcasted_iota(jnp.int32, (ROWS, ROWS), 0) // (2 * QUAD)
    half_k = lax.broadcasted_iota(jnp.int32, (ROWS, ROWS), 1) // (2 * QUAD)
    allowed = jnp.logical_or(half_q == half_k, i != lat_size - 1)
    first = lax.broadcasted_iota(jnp.int32, (ROWS, HD2), 1) < HD2 // 2
    inv_root = (HD2 // 2) ** -0.5

    def of_head(values, h):
        return jnp.where(first if h % 2 == 0 else jnp.logical_not(first), values, jnp.zeros_like(values))

    def attend(pair):
        at_q = slice(HD2 * pair, HD2 * (pair + 1))
        at_k = slice(D + HD2 * pair, D + HD2 * (pair + 1))
        at_v = slice(2 * D + HD2 * pair, 2 * D + HD2 * (pair + 1))
        q, k, v = proj[:, at_q], proj[:, at_k], proj[:, at_v]
        results = []
        for h in (2 * pair, 2 * pair + 1):
            scores = dot(of_head(q, h), k, NT) * inv_root + bias[h]
            scores = jnp.where(allowed, scores, FAR)
            weights = jnp.exp(scores - jnp.max(scores, axis=-1, keepdims=True))
            weights = weights / jnp.sum(weights, axis=-1, keepdims=True)
            att[h] = weights
            results.append(dot(weights.astype(BF16), v))
        return jnp.where(first, results[0], results[1]).astype(BF16)

    attended = [attend(0), attend(1)]

    z_arrive(merge_z)
    merge_x = push(merge_w.at[y, :, xh], merge_w.at[y, :, xh], at(y, z, other), j)
    arrive([split_x])

    def y_spread(whole):
        return [push(whole.at[y], whole.at[y], at(y_by(d), z, xh), j) for d in (1, -1)]

    split_y = y_spread(split_w)

    attended += [attend(2), attend(3)]
    attended = jnp.concatenate(attended, axis=1)
    y_rolled = (rolled + dot(attended, outer[...])).astype(BF16)
    y_out[...] = y_rolled.reshape(4, QUAD, D)
    y_in[3] = y_out[0]
    y_move = roll_out(y_out, y_in)

    arrive([merge_x])
    merge_y = y_spread(merge_w)

    row = lax.broadcasted_iota(jnp.int32, (D, D), 0)
    col = lax.broadcasted_iota(jnp.int32, (D, D), 1)
    block = col // (4 * Z)
    want = ((block // XH) * Z + (col // 4) % Z) * (4 * XH) + (block % XH) * 4 + col % 4
    swap = (row == want).astype(F32).astype(BF16)
    toks = dot(dense[...], normed[...]).astype(BF16)
    toks_all[j] = dot(toks, swap).astype(BF16)
    toks_move = [push(toks_all.at[j], toks_all.at[j], i, lon_by(d)) for d in range(1, lon_size)]

    arrive(y_move)
    y_pairs = lanes(dot(pair_of_quarter[...], y_in[...].reshape(ROWS, D)))
    pair_unit, pair_scale = norm_parts(y_pairs)
    norm_all[j] = (pair_unit * merge_gain[...]).astype(BF16)
    norm_move = [push(norm_all.at[j], norm_all.at[j], i, lon_by(d)) for d in range(1, lon_size)]

    def y_forward(whole, halves):
        return [
            push(halves(whole, y_by(-1), 0), halves(whole, y_by(-1), 0), at(y_by(1), z, xh), j),
            push(halves(whole, y_by(1), 1), halves(whole, y_by(1), 1), at(y_by(-1), z, xh), j),
        ]

    arrive(split_y)
    split_f = y_forward(split_w, lambda w, yy, part: w.at[yy, part])
    arrive(merge_y)
    merge_f = y_forward(merge_w, lambda w, yy, part: w.at[yy, pl.ds(part * (Z // 2), Z // 2)])

    arrive(cot_move)
    arrive(split_f)

    def split_block(k):
        return split_w[:, :, k].reshape(MS, MS)

    cots = cot_all[...].reshape(lon_size * QUAD, 4 * D)
    grad_merged = dot(cots[:, :MS], split_block(0), NT)
    for k in range(1, KB):
        grad_merged = grad_merged + dot(cots[:, MS * k : MS * (k + 1)], split_block(k), NT)
    grad_merged = grad_merged.astype(BF16)
    arrive(merge_f)
    merge_full = merge_w[...].reshape(4 * D, MS)
    gm_out[...] = dot(grad_merged, merge_full, NT).astype(BF16).reshape(lon_size, QUAD, 4 * D)

    def scatter(src, dst):
        return [push(src.at[lon_by(d)], dst.at[j], i, lon_by(d)) for d in range(1, lon_size)]

    def total(mine, received):
        result = mine[j].astype(F32)
        for d in range(1, lon_size):
            result = result + received[lon_by(-d)].astype(F32)
        return result

    gm_move = scatter(gm_out, gm_in)

    arrive(norm_move)
    merged = dot(norm_all[...].reshape(lon_size * QUAD, 4 * D), merge_full).astype(BF16)
    for k in range(KB):
        part = dot(merged, split_block(k)).astype(BF16)
        so_out[:, :, MS * k : MS * (k + 1)] = part.reshape(lon_size, QUAD, MS)

    arrive(gm_move)
    grad_mnorm = total(gm_out, gm_in)
    grad_y = cot_all[j].astype(F32) + norm_back(pair_unit, pair_scale, grad_mnorm, merge_gain[...])
    grad_y = dot(pair_of_quarter[...], stacked(grad_y.astype(BF16)), TN).astype(BF16)
    gy_out[...] = grad_y.reshape(4, QUAD, D)
    gy_in[0] = gy_out[3]
    gy_move = roll_in(gy_out, gy_in)
    so_move = scatter(so_out, so_in)

    arrive(gy_move)
    grad_rolled_y = gy_in[...].reshape(ROWS, D)
    grad_attended = dot(grad_rolled_y, outer[...], NT).astype(BF16)
    for pair in range(HEADS // 2):
        at_q = slice(HD2 * pair, HD2 * (pair + 1))
        at_k = slice(D + HD2 * pair, D + HD2 * (pair + 1))
        at_v = slice(2 * D + HD2 * pair, 2 * D + HD2 * (pair + 1))
        q, k, v = proj[:, at_q], proj[:, at_k], proj[:, at_v]
        g = grad_attended[:, at_q]
        found = []
        for h in (2 * pair, 2 * pair + 1):
            weights = att[h]
            grad_p = dot(of_head(g, h), v, NT)
            grad_v = dot(weights.astype(BF16), g, TN)
            shared = jnp.sum(weights * grad_p, axis=-1, keepdims=True)
            grad_s = (weights * (grad_p - shared)).astype(BF16)
            found.append((dot(grad_s, k) * inv_root, dot(grad_s, q, TN) * inv_root, grad_v))
        for where, even, odd in zip((at_q, at_k, at_v), *found):
            gp[:, where] = jnp.where(first, even, odd).astype(BF16)
    few = dot(dense[...], gp[...]).astype(BF16)
    for d in range(lon_size):
        gp_out[d] = few[:, CW * d : CW * (d + 1)]
    gp_move = scatter(gp_out, gp_in)
    gp_in[j] = gp_out[j]

    grad_normed = dot(gp[...], inner[...], NT)
    grad_in = grad_rolled_y.astype(F32) + norm_back(unit_keep[...], scale, grad_normed, gain[...])
    gf_out[...] = grad_in.astype(BF16).reshape(4, QUAD, D)
    gf_in[3] = gf_out[0]
    gf_move = roll_out(gf_out, gf_in)

    arrive(toks_move)
    arrive(gp_move)
    tokens = lon_size * WIN
    summed = dot(toks_all[...].reshape(tokens, D), gp_in[...].reshape(tokens, CW), TN)
    dw_out[...] = summed.astype(BF16).reshape(Y * XH, 4 * Z, CW)
    dw_move = []
    for dy, dx in plane:
        yy, xx = y_by(dy), lax.rem(xh + dx, XH)
        dw_move.append(push(dw_out.at[yy * XH + xx], dw_in.at[y * XH + xh], at(yy, z, xx), j))

    def from_pairs(wide):
        return dot(to_pair[...], stacked(wide), TN).astype(BF16)

    def put(dst, rows):
        for l in range(LEVELS):
            for r in range(WIN_LAT):
                start = (l * WIN_LAT + r) * 16
                dst[l, r] = rows[start : start + WIN_LON]

    arrive(so_move)
    put(outputs, from_pairs((y_pairs + total(so_out, so_in)).astype(BF16)))

    arrive(dw_move)
    mine = dw_out[y * XH + xh].astype(F32)
    for dy, dx in plane:
        slot = y_by(-dy) * XH + lax.rem(xh + dx, XH)
        mine = mine + dw_in[slot].astype(F32)
    mine = mine.astype(BF16)
    CB = CW // 3
    tall = jnp.concatenate([mine[:, CB * c : CB * (c + 1)] for c in range(3)], axis=0)
    row = lax.broadcasted_iota(jnp.int32, (16 * Z, 12 * Z), 0)
    col = lax.broadcasted_iota(jnp.int32, (16 * Z, 12 * Z), 1)
    inner_row = row % 16
    want = (inner_row // 4) * (4 * Z) + (row // 16) * 4 + inner_row % 4
    spread = jnp.logical_and(col == want, inner_row < 12).astype(F32).astype(BF16)
    z_out[...] = dot(spread, tall).astype(BF16).reshape(Z, 16, CB)
    z_start(sums_z)
    z_in[z] = z_out[z]

    arrive(gf_move)
    put(grad_fields, dot(to_quarter[...], gf_in[...].reshape(ROWS, D), TN).astype(BF16))

    z_arrive(sums_z)
    owned = jnp.sum(z_in[...].astype(F32), axis=0)
    shrink = 1.0 / math.sqrt(WIN * lat_size * lon_size)
    for c in range(3):
        grad_inner[:, CB * c : CB * (c + 1)] = owned[4 * c : 4 * c + 4] * shrink

    for copy in sent:
        copy.wait_send()

    @pl.loop(1, Z)
    def _(d):
        split_z(d).wait_send()
        merge_z(d).wait_send()
        sums_z(d).wait_send()


def local(
    lon_size, fields, cotangent, norm_gain, inner_weight, outer_weight, bias_table, merge_gain,
    merge_weight, split_weight,
):
    D = fields.shape[-1]
    to_quarter, to_pair, pair_of_quarter, dense, pick = (jnp.asarray(a) for a in orders())
    middle = (RELS - 1) // 2
    wrapped = jnp.concatenate(
        [
            bias_table[:, middle::-1],
            jnp.zeros((HEADS, 2 * SPAN - RELS), F32),
            bias_table[:, :middle:-1],
        ],
        axis=1,
    )
    vmem = pl.BlockSpec(memory_space=pltpu.VMEM)
    bias = pl.pallas_call(
        bias_kernel,
        out_shape=jax.ShapeDtypeStruct((HEADS, ROWS, ROWS), F32),
        in_specs=[vmem] * 2,
        out_specs=vmem,
        compiler_params=pltpu.CompilerParams(vmem_limit_bytes=32 * 1024 * 1024),
    )(wrapped, pick)
    MS, CW = D // 2, 3 * D // lon_size

    def buf(*shape, dtype=BF16):
        return pltpu.VMEM(shape, dtype)

    quarters = (4, QUAD, D)
    wide = (lon_size, QUAD, 4 * D)
    scratch = [
        buf(ROWS, D), buf(*quarters), buf(*quarters), buf(*wide), buf(*wide),
        buf(Z, 16, MS), buf(64, MS, dtype=F32), buf(Y, XH, 8, 2 * Z, MS), buf(Y, Z, XH, 16, MS),
        buf(*quarters), buf(*quarters), buf(*wide), buf(*wide), buf(*quarters), buf(*quarters),
        buf(*quarters), buf(*quarters), buf(HEADS, ROWS, ROWS, dtype=F32), buf(ROWS, 3 * D),
        buf(ROWS, D),
        buf(lon_size, WIN, D), buf(ROWS, 3 * D), buf(lon_size, WIN, CW), buf(lon_size, WIN, CW),
        buf(Y * XH, 4 * Z, CW), buf(Y * XH, 4 * Z, CW), buf(Z, 16, CW // 3), buf(Z, 16, CW // 3),
        buf(*wide), buf(*wide), buf(ROWS, D, dtype=F32),
    ]
    count = 4 * 3 + 6 * (lon_size - 1) + 2 * 5 + (Y * XH - 1)
    scratch += [
        pltpu.SemaphoreType.DMA((count,)), pltpu.SemaphoreType.DMA((count,)),
        pltpu.SemaphoreType.DMA((3, Z)), pltpu.SemaphoreType.DMA((3, Z)),
    ]
    return pl.pallas_call(
        functools.partial(main_kernel, lon_size),
        out_shape=(
            jax.ShapeDtypeStruct(fields.shape, BF16),
            jax.ShapeDtypeStruct(fields.shape, BF16),
            jax.ShapeDtypeStruct((4, CW), F32),
        ),
        in_specs=[vmem] * 13,
        out_specs=(vmem,) * 3,
        scratch_shapes=scratch,
        compiler_params=pltpu.CompilerParams(
            collective_id=0, has_side_effects=True, vmem_limit_bytes=48 * 1024 * 1024
        ),
    )(
        fields, cotangent, norm_gain.reshape(1, D), inner_weight, outer_weight, bias,
        merge_gain.reshape(1, 4 * D), merge_weight, split_weight,
        to_quarter, to_pair, pair_of_quarter, dense,
    )


def solution(mesh):
    return jax.shard_map(
        functools.partial(local, mesh.shape["lon"]),
        mesh=mesh,
        in_specs=(
            P(None, "lat", "lon", None),
            P(None, "lat", "lon", None),
            P(),
            P(),
            P(),
            P(),
            P(),
            P("lat", None),
            P("lat", None),
        ),
        out_specs=(P(None, "lat", "lon", None), P(None, "lat", "lon", None), P("lat", "lon")),
        check_vma=False,
    )
```

time: 1910 us -> 112 us (0.06)
  waiting for transfers between devices: 1740 us -> 0 us
  Pallas kernels: 0 us -> 103 us
  local copies, waits for them, and re-layouts: 66.9 us -> 7.33 us
  starting transfers between devices: 49.7 us -> 0 us
  matrix products: 25.4 us -> 0 us
    unnamed x6 -> x0, waiting for transfers between devices: 1380 us -> none
    all_gather x2 -> x0, waiting for transfers between devices: 341 us -> none  [the longest x1 223 us: local(): lax.all_gather(merge_weight, 'lat', axis=0, tiled=True)]
    pallas_call x0 -> x2, Pallas kernels: none -> 103 us  [the longest x1 99.1 us: local(): pl.pallas_call(functools.partial(main_kernel, lon_size), out_shape=(jax.S...]
    gather x2 -> x0, local copies, waits for them, and re-layouts: 49.9 us -> none  [local(): pos_bias = jnp.take(bias_table, relative_index(), axis=1)]
    ppermute x8 -> x0, starting transfers between devices: 49.6 us -> none  [passed_along(): lax.ppermute(value, axis, [(i, (i + by) % peers) for i in range(peers)])]
    dot_general x13 -> x0, matrix products: 25.4 us -> none  [the longest x1 6.9 us: local(): lax.dot_general(grad_merged, full_merge, contract_last, preferred_element...]
  transfers between devices with their start and end apart: 12 -> 0, of which waited for: 9 -> 0; matrix products, arithmetic and copies ran while one was open for 4% -> 0% of each run, Pallas kernels for 0% -> 0%
where the time goes in v1:
time: 112 us
  Pallas kernels  103 us (92%)
  local copies, waits for them, and re-layouts  7.33 us (7%)
    pallas_call x1, Pallas kernels, local(): pl.pallas_call(functools.partial(main_kernel, lon_size), out_shape=(jax.S...  99.1 us
    pallas_call x1, Pallas kernels, local(): pl.pallas_call(bias_kernel, out_shape=jax.ShapeDtypeStruct((HEADS, ROWS,...  4.17 us
    unnamed x29, local copies, waits for them, and re-layouts  4 us

profile of v1, /device:TPU:1, one launch (start us, length us, event | category | flops | bytes accessed | tf_op | source)
XLA Modules:
  0.0 111.5 jit_solution(10404252709173856691)
XLA Ops:
  0.7 0.1 pad.1.clone
  0.7 0.9 slice.7
  1.7 0.2 reverse
  1.9 0.1 slice.8
  1.9 0.7 slice.6
  2.7 0.2 reverse.1
  2.9 0.1 slice.9
  3.0 0.1 pad_maximum_fusion.wrapped_ref
  3.0 0.9 copy.17.fields
  4.0 0.9 copy.18.cotangent
  4.9 0.0 copy-start.2
  4.9 0.9 copy-done.2
  5.8 0.0 copy-start.7
  5.8 0.0 copy-start.8
  5.9 0.0 copy-start.9
  5.9 0.0 copy-start.10
  5.9 4.2 %shard_map.157.bias = f32[8,192,192]{2,1,0:T(8,128)S(1)} custom-call(f32[8,768]{1,0:T(8,128)S(1)} %pad_maximum_fusion.wrapped_ref, bf16[192,384]{1,0:T(8,128)(2,1)S(1)} %copy-done.2), custom_call_target="tpu_custom_call" | custom-call | tf_op jit(solution)/shard_map/pallas_call | solution.py:473
  10.1 0.0 copy-done.1
  10.1 0.0 copy-done
  10.1 0.0 copy-done.3
  10.2 99.1 %shard_map.158 = (bf16[2,6,12,512]{3,2,1,0:T(8,128)(2,1)S(1)}, bf16[2,6,12,512]{3,2,1,0:T(8,128)(2,1)S(1)}, f32[4,384]{1,0:T(4,128)S(1)}) custom-call(bf16[2,6,12,512]{3,2,1,0:T(8,128)(2,1)S(1)} %copy.17.fields, bf16[2,6,12,512]{3,2,1,0:T(8,128)(2,1)S(1)} %copy.18.cotangent, f32[1,512]{1,0:T(1,128)S(1)} %bitcast.5, bf16[512,1536]{1,0:T(8,128)(2,1)S(1)} %copy-done, ...), custom_call_target="tpu_custom_call" | custom-call | tf_op jit(solution)/shard_map/pallas_call | solution.py:502
  109.3 0.8 copy.19
  110.1 0.8 copy.20
  110.9 0.6 copy.22
  (14 shorter events, 0.0 us)
Async XLA Ops:
  0.6 9.4 %copy-start.1 = (bf16[512,512]{1,0:T(8,128)(2,1)S(1)}, bf16[512,512]{1,0:T(8,128)(2,1)}, u32[]{:S(2)}) copy-start(bf16[512,512]{1,0:T(8,128)(2,1)} %outer.1) | copy-start | bytes 1572868
  0.6 9.4 %copy-start = (bf16[512,1536]{1,0:T(8,128)(2,1)S(1)}, bf16[512,1536]{1,0:T(8,128)(2,1)}, u32[]{:S(2)}) copy-start(bf16[512,1536]{1,0:T(8,128)(2,1)} %inner.1) | copy-start | bytes 4718596
  4.9 0.9 copy-start.2
  5.8 4.3 %copy-start.3 = (bf16[192,192]{1,0:T(8,128)(2,1)S(1)}, bf16[192,192]{1,0:T(8,128)(2,1)}, u32[]{:S(2)}) copy-start(bf16[192,192]{1,0:T(8,128)(2,1)} %constant.14.clone.pair_of_quarter) | copy-start | bytes 221188
  5.8 4.3 %copy-start.4 = (bf16[192,192]{1,0:T(8,128)(2,1)S(1)}, bf16[192,192]{1,0:T(8,128)(2,1)}, u32[]{:S(2)}) copy-start(bf16[192,192]{1,0:T(8,128)(2,1)} %constant.13.clone.to_pair) | copy-start | bytes 221188
  5.8 4.3 %copy-start.5 = (bf16[192,192]{1,0:T(8,128)(2,1)S(1)}, bf16[192,192]{1,0:T(8,128)(2,1)}, u32[]{:S(2)}) copy-start(bf16[192,192]{1,0:T(8,128)(2,1)} %constant.12.clone.to_quarter) | copy-start | bytes 221188
  5.8 4.3 %copy-start.6 = (bf16[144,192]{1,0:T(8,128)(2,1)S(1)}, bf16[144,192]{1,0:T(8,128)(2,1)}, u32[]{:S(2)}) copy-start(bf16[144,192]{1,0:T(8,128)(2,1)} %constant.15.clone.dense) | copy-start | bytes 165892
  5.8 4.3 %copy-start.7 = (bf16[16,1024]{1,0:T(8,128)(2,1)S(1)}, bf16[16,1024]{1,0:T(8,128)(2,1)}, u32[]{:S(2)}) copy-start(bf16[16,1024]{1,0:T(8,128)(2,1)} %merge_shard.1) | copy-start | bytes 98308
  5.8 4.3 %copy-start.8 = (bf16[8,2048]{1,0:T(8,128)(2,1)S(1)}, bf16[8,2048]{1,0:T(8,128)(2,1)}, u32[]{:S(2)}) copy-start(bf16[8,2048]{1,0:T(8,128)(2,1)} %split_shard.1) | copy-start | bytes 98308
  5.9 4.3 %copy-start.9 = (f32[2048]{0:T(1024)S(1)}, f32[2048]{0:T(1024)}, u32[]{:S(2)}) copy-start(f32[2048]{0:T(1024)} %param.20) | copy-start | bytes 24580
  5.9 4.3 %copy-start.10 = (f32[512]{0:T(512)S(1)}, f32[512]{0:T(512)}, u32[]{:S(2)}) copy-start(f32[512]{0:T(512)} %param.16) | copy-start | bytes 6148

commit v2 on v1

--- a/solution.py
+++ b/solution.py
@@ -39,14 +39,14 @@
         for r in range(WIN_LAT):
             for c in range(WIN_LON):
                 token = (l, r, c)
-                natural[token] = (l * WIN_LAT + r) * 16 + c
+                natural[token] = (r * WIN_LON + c) * LEVELS + l
                 inside = (l * 3 + r % 3) * 6 + c % 6
                 quarter[token] = ((r // 3) * 2 + c // 6) * QUAD + inside
                 compact[token] = ((r // 3) * 2 + c // 6) * 36 + inside
                 pair[token] = ((r % 2) * 2 + c % 2) * QUAD + (l * 3 + r // 2) * 6 + c // 2
                 base[token] = (l * (2 * WIN_LAT - 1) + r) * (2 * WIN_LON - 1) + c
-    to_quarter = np.zeros((ROWS, ROWS), ml_dtypes.bfloat16)
-    to_pair = np.zeros((ROWS, ROWS), ml_dtypes.bfloat16)
+    to_quarter = np.zeros((ROWS, WIN), ml_dtypes.bfloat16)
+    to_pair = np.zeros((ROWS, WIN), ml_dtypes.bfloat16)
     pair_of_quarter = np.zeros((ROWS, ROWS), ml_dtypes.bfloat16)
     dense = np.zeros((WIN, ROWS), ml_dtypes.bfloat16)
     pick = np.zeros((ROWS, SPAN), ml_dtypes.bfloat16)
@@ -59,19 +59,23 @@
     return to_quarter, to_pair, pair_of_quarter, dense, pick
 
 
-def bias_kernel(wrapped_ref, pick_ref, bias_ref):
-    pick = pick_ref[...]
+def make_bias(table_ref, padded_ref, pick, bias_ref):
+    middle = (RELS - 1) // 2
+    padded_ref[...] = jnp.zeros((HEADS, 2 * SPAN), F32)
+    padded_ref[:, :RELS] = table_ref[...]
+    back = 2 * SPAN - middle
+    padded_ref[...] = pltpu.roll(padded_ref[...], back % 128, 1)
     used = jnp.sum(dot(jnp.ones((8, SPAN), BF16), pick, NT), axis=0, keepdims=True) > 0.5
     for h in range(HEADS):
-        row = jnp.broadcast_to(wrapped_ref[h : h + 1, :], (SPAN, 2 * SPAN))
-        shifted = pltpu.roll(row, 0, 1, stride=1, stride_axis=0)[:, :SPAN]
+        row = jnp.broadcast_to(padded_ref[h : h + 1, :], (SPAN, 2 * SPAN))
+        shifted = pltpu.roll(row, back // 128 * 128, 1, stride=1, stride_axis=0)[:, :SPAN]
         high = shifted.astype(BF16)
         rest = shifted - high.astype(F32)
-        middle = rest.astype(BF16)
-        low = (rest - middle.astype(F32)).astype(BF16)
+        middle_part = rest.astype(BF16)
+        low = (rest - middle_part.astype(F32)).astype(BF16)
         total = jnp.zeros((ROWS, ROWS), F32)
-        for part in (low, middle, high):
-            total = total + dot(dot(pick, part).astype(BF16), pick, NT)
+        for part in (low, middle_part, high):
+            total = total + dot(dot(pick, part, NT).astype(BF16), pick, NT)
         bias_ref[h] = jnp.where(used, total, FAR)
 
 
@@ -92,14 +96,34 @@
 
 def main_kernel(
     lon_size,
-    fields, cotangent, gain, inner, outer, bias, merge_gain, merge_shard, split_shard,
-    to_quarter, to_pair, pair_of_quarter, dense,
-    outputs, grad_fields, grad_inner,
-    nat, quads, win, cot_all, norm_all, raw, stack, split_w, merge_w,
-    y_out, y_in, gm_out, gm_in, gy_out, gy_in, gf_out, gf_in, att, proj, normed,
-    toks_all, gp, gp_out, gp_in, dw_out, dw_in, z_out, z_in, so_out, so_in, unit_keep,
-    ssem, rsem, zsend, zrecv,
+    *refs,
 ):
+    operands, refs = refs[:14], refs[14:]
+    (
+        outputs, grad_fields, grad_inner,
+        nat, quads, win, cot_all, norm_all, raw, stack, split_w, merge_w,
+        y_out, y_in, gm_out, gy_out, gy_in, gf_out, gf_in, att, proj, normed,
+        toks_all, gp, gp_out, gp_in, dw_out, dw_in, z_out, z_in, so_out, unit_keep,
+        bias, padded, gp_mid, gm_mid, so_mid, cross_out, cross_in,
+        ssem, rsem, zsend, zrecv, lsem,
+        *local_refs,
+    ) = refs
+    loads = [
+        pltpu.make_async_copy(src, dst, lsem.at[k])
+        for k, (src, dst) in enumerate(zip(operands, local_refs))
+    ]
+    for load in loads:
+        load.start()
+    (
+        fields, to_quarter, split_shard, merge_shard, cotangent, to_pair, gain, inner, table,
+        pick, outer, pair_of_quarter, merge_gain, dense,
+    ) = local_refs
+    loads = dict(zip(map(id, local_refs), loads))
+
+    def ready(*wanted):
+        for ref in wanted:
+            loads[id(ref)].wait()
+
     D = fields.shape[-1]
     MS = D // 2
     CW = 3 * D // lon_size
@@ -110,6 +134,10 @@
     xh = lax.rem(i, XH)
     z = lax.rem(i // XH, Z)
     y = i // (XH * Z)
+    other = lax.rem(xh + 1, XH)
+    mate = j + 1 - 2 * lax.rem(j, 2)
+    across = lax.rem(j + 2, lon_size)
+    beyond = lax.rem(mate + 2, lon_size)
 
     def at(yy, zz, xx):
         return (yy * Z + zz) * XH + xx
@@ -142,29 +170,6 @@
     def arrive(copies):
         for copy in copies:
             copy.wait_recv()
-
-    def to_natural(src):
-        nat[...] = jnp.zeros((ROWS, D), BF16)
-        for l in range(LEVELS):
-            for r in range(WIN_LAT):
-                start = (l * WIN_LAT + r) * 16
-                nat[start : start + WIN_LON, :] = src[l, r]
-        return nat[...]
-
-    quads[...] = dot(to_quarter[...], to_natural(fields)).astype(BF16).reshape(4, QUAD, D)
-    win[0] = quads[3]
-
-    for k in range(KB):
-        stack[8 * k : 8 * k + 8, :] = split_shard[:, MS * k : MS * (k + 1)].astype(F32)
-    row = lax.broadcasted_iota(jnp.int32, (16, 64), 0)
-    col = lax.broadcasted_iota(jnp.int32, (16, 64), 1)
-    sel = (col == (row // 2) * 8 + 2 * j + row % 2).astype(F32).astype(BF16)
-    raw[z] = dot(sel, stack[...].astype(BF16)).astype(BF16)
-    own = lax.broadcasted_iota(jnp.int32, (2 * D, MS), 1)
-    place = ((own // (2 * Z * XH)) * Z + (own // 2) % Z) * XH + (own // (2 * Z)) % XH
-    col = lax.broadcasted_iota(jnp.int32, (2 * D, MS), 0)
-    sel = (col == 8 * place + 2 * j + own % 2).astype(F32).astype(BF16)
-    merge_w[y, z, xh] = dot(merge_shard[...], sel).astype(BF16)
 
     partners = []
     for a, b in ((0, 1), (1, 0), (1, 1)):
@@ -184,6 +189,30 @@
             barrier, inc=1, device_id=(at(y, z_by(d), xh), j), device_id_type=MESH
         )
 
+    def to_natural(src):
+        for r in range(WIN_LAT):
+            for c in range(WIN_LON):
+                start = (r * WIN_LON + c) * LEVELS
+                nat[start : start + LEVELS, :] = src[r, c]
+        return nat[...]
+
+    ready(fields, to_quarter)
+    quads[...] = dot(to_quarter[...], to_natural(fields)).astype(BF16).reshape(4, QUAD, D)
+    win[0] = quads[3]
+
+    ready(split_shard, merge_shard)
+    for k in range(KB):
+        stack[8 * k : 8 * k + 8, :] = split_shard[:, MS * k : MS * (k + 1)].astype(F32)
+    row = lax.broadcasted_iota(jnp.int32, (16, 64), 0)
+    col = lax.broadcasted_iota(jnp.int32, (16, 64), 1)
+    sel = (col == (row // 2) * 8 + 2 * j + row % 2).astype(F32).astype(BF16)
+    raw[z] = dot(sel, stack[...].astype(BF16)).astype(BF16)
+    own = lax.broadcasted_iota(jnp.int32, (1, MS), 1)
+    place = ((own // (2 * Z * XH)) * Z + (own // 2) % Z) * XH + (own // (2 * Z)) % XH
+    col = lax.broadcasted_iota(jnp.int32, (2 * D, MS), 0)
+    sel = (col == 8 * place + 2 * j + own % 2).astype(F32).astype(BF16)
+    merge_w[y, z, xh] = dot(merge_shard[...], sel).astype(BF16)
+
     pl.semaphore_wait(barrier, len(partners) + Z - 1)
 
     def roll_in(src, dst):
@@ -224,37 +253,71 @@
             make(d).wait_recv()
 
     fields_move = roll_in(quads, win)
+
     z_start(split_z)
     z_start(merge_z)
 
+    def gather_start(whole):
+        mine = whole.at[j]
+        return push(mine, mine, i, across), push(mine, mine, i, mate)
+
+    def gather_relay(whole, started):
+        arrive(started[:1])
+        came = whole.at[across]
+        return started[1], push(came, came, i, mate)
+
+    def reduce_start(src, mid):
+        return push(src.at[mate], mid.at[0], i, mate), push(src.at[beyond], mid.at[1], i, mate)
+
+    def reduce_cross(src, mid, started, slot):
+        arrive(started)
+        cross_out[slot] = (src[across].astype(F32) + mid[1].astype(F32)).astype(BF16)
+        return [push(cross_out.at[slot], cross_in.at[slot], i, across)]
+
+    def reduce_end(src, mid, crossed, slot):
+        arrive(crossed)
+        return src[j].astype(F32) + mid[0].astype(F32) + cross_in[slot].astype(F32)
+
     def lanes(rows):
         return jnp.concatenate([rows[QUAD * s : QUAD * (s + 1)] for s in range(4)], axis=1)
 
     def stacked(wide):
         return jnp.concatenate([wide[:, D * s : D * (s + 1)] for s in range(4)], axis=0)
 
+    ready(cotangent, to_pair)
     cot_all[j] = lanes(dot(to_pair[...], to_natural(cotangent)).astype(BF16))
-    cot_move = [push(cot_all.at[j], cot_all.at[j], i, lon_by(d)) for d in range(1, lon_size)]
 
     arrive(fields_move)
     rolled = win[...].reshape(ROWS, D).astype(F32)
+    ready(gain, inner)
     unit, scale = norm_parts(rolled)
     unit_keep[...] = unit
     normed[...] = (unit * gain[...]).astype(BF16)
     proj[...] = dot(normed[...], inner[...]).astype(BF16)
 
-    z_arrive(split_z)
+    ready(table, pick)
+    make_bias(table, padded, pick[...], bias)
+
     full = Z * 16
-    out = lax.broadcasted_iota(jnp.int32, (full, full), 0)
+    out = lax.broadcasted_iota(jnp.int32, (full, 1), 0)
     src = lax.broadcasted_iota(jnp.int32, (full, full), 1)
     want = ((out % (2 * Z)) // 2) * 16 + (out // (2 * Z)) * 2 + out % 2
     regroup = (src == want).astype(F32).astype(BF16)
+    z_arrive(split_z)
     split_w[y, xh] = dot(regroup, raw[...].reshape(full, MS)).astype(BF16).reshape(KB, 2 * Z, MS)
-    other = lax.rem(xh + 1, XH)
     split_x = push(split_w.at[y, xh], split_w.at[y, xh], at(y, z, other), j)
-
-    half_q = lax.broadcasted_iota(jnp.int32, (ROWS, ROWS), 0) // (2 * QUAD)
-    half_k = lax.broadcasted_iota(jnp.int32, (ROWS, ROWS), 1) // (2 * QUAD)
+    z_arrive(merge_z)
+    merge_x = push(merge_w.at[y, :, xh], merge_w.at[y, :, xh], at(y, z, other), j)
+
+    def y_spread(whole):
+        return [push(whole.at[y], whole.at[y], at(y_by(d), z, xh), j) for d in (1, -1)]
+
+    arrive([split_x])
+    split_y = y_spread(split_w)
+    cot_move = gather_start(cot_all)
+
+    half_q = lax.broadcasted_iota(jnp.int32, (ROWS, 1), 0) // (2 * QUAD)
+    half_k = lax.broadcasted_iota(jnp.int32, (1, ROWS), 1) // (2 * QUAD)
     allowed = jnp.logical_or(half_q == half_k, i != lat_size - 1)
     first = lax.broadcasted_iota(jnp.int32, (ROWS, HD2), 1) < HD2 // 2
     inv_root = (HD2 // 2) ** -0.5
@@ -279,39 +342,26 @@
 
     attended = [attend(0), attend(1)]
 
-    z_arrive(merge_z)
-    merge_x = push(merge_w.at[y, :, xh], merge_w.at[y, :, xh], at(y, z, other), j)
-    arrive([split_x])
-
-    def y_spread(whole):
-        return [push(whole.at[y], whole.at[y], at(y_by(d), z, xh), j) for d in (1, -1)]
-
-    split_y = y_spread(split_w)
+    arrive([merge_x])
+    merge_y = y_spread(merge_w)
+
+    row = lax.broadcasted_iota(jnp.int32, (D, D), 0)
+    col = lax.broadcasted_iota(jnp.int32, (1, D), 1)
+    block = col // (4 * Z)
+    want = ((block // XH) * Z + (col // 4) % Z) * (4 * XH) + (block % XH) * 4 + col % 4
+    swap = (row == want).astype(F32).astype(BF16)
+    ready(dense)
+    toks = dot(dense[...], normed[...]).astype(BF16)
+    toks_all[j] = dot(toks, swap).astype(BF16)
+    toks_move = gather_start(toks_all)
 
     attended += [attend(2), attend(3)]
     attended = jnp.concatenate(attended, axis=1)
+    ready(outer)
     y_rolled = (rolled + dot(attended, outer[...])).astype(BF16)
     y_out[...] = y_rolled.reshape(4, QUAD, D)
     y_in[3] = y_out[0]
     y_move = roll_out(y_out, y_in)
-
-    arrive([merge_x])
-    merge_y = y_spread(merge_w)
-
-    row = lax.broadcasted_iota(jnp.int32, (D, D), 0)
-    col = lax.broadcasted_iota(jnp.int32, (D, D), 1)
-    block = col // (4 * Z)
-    want = ((block // XH) * Z + (col // 4) % Z) * (4 * XH) + (block % XH) * 4 + col % 4
-    swap = (row == want).astype(F32).astype(BF16)
-    toks = dot(dense[...], normed[...]).astype(BF16)
-    toks_all[j] = dot(toks, swap).astype(BF16)
-    toks_move = [push(toks_all.at[j], toks_all.at[j], i, lon_by(d)) for d in range(1, lon_size)]
-
-    arrive(y_move)
-    y_pairs = lanes(dot(pair_of_quarter[...], y_in[...].reshape(ROWS, D)))
-    pair_unit, pair_scale = norm_parts(y_pairs)
-    norm_all[j] = (pair_unit * merge_gain[...]).astype(BF16)
-    norm_move = [push(norm_all.at[j], norm_all.at[j], i, lon_by(d)) for d in range(1, lon_size)]
 
     def y_forward(whole, halves):
         return [
@@ -321,10 +371,19 @@
 
     arrive(split_y)
     split_f = y_forward(split_w, lambda w, yy, part: w.at[yy, part])
+    cot_rest = gather_relay(cot_all, cot_move)
+
+    arrive(y_move)
+    ready(pair_of_quarter, merge_gain)
+    y_pairs = lanes(dot(pair_of_quarter[...], y_in[...].reshape(ROWS, D)))
+    pair_unit, pair_scale = norm_parts(y_pairs)
+    norm_all[j] = (pair_unit * merge_gain[...]).astype(BF16)
+    norm_move = gather_start(norm_all)
+
     arrive(merge_y)
     merge_f = y_forward(merge_w, lambda w, yy, part: w.at[yy, pl.ds(part * (Z // 2), Z // 2)])
 
-    arrive(cot_move)
+    arrive(cot_rest)
     arrive(split_f)
 
     def split_block(k):
@@ -339,31 +398,24 @@
     merge_full = merge_w[...].reshape(4 * D, MS)
     gm_out[...] = dot(grad_merged, merge_full, NT).astype(BF16).reshape(lon_size, QUAD, 4 * D)
 
-    def scatter(src, dst):
-        return [push(src.at[lon_by(d)], dst.at[j], i, lon_by(d)) for d in range(1, lon_size)]
-
-    def total(mine, received):
-        result = mine[j].astype(F32)
-        for d in range(1, lon_size):
-            result = result + received[lon_by(-d)].astype(F32)
-        return result
-
-    gm_move = scatter(gm_out, gm_in)
-
-    arrive(norm_move)
-    merged = dot(norm_all[...].reshape(lon_size * QUAD, 4 * D), merge_full).astype(BF16)
-    for k in range(KB):
-        part = dot(merged, split_block(k)).astype(BF16)
-        so_out[:, :, MS * k : MS * (k + 1)] = part.reshape(lon_size, QUAD, MS)
-
-    arrive(gm_move)
-    grad_mnorm = total(gm_out, gm_in)
+    gm_start = reduce_start(gm_out, gm_mid)
+    gm_crossed = reduce_cross(gm_out, gm_mid, gm_start, 0)
+    norm_rest = gather_relay(norm_all, norm_move)
+    toks_rest = gather_relay(toks_all, toks_move)
+
+    grad_mnorm = reduce_end(gm_out, gm_mid, gm_crossed, 0)
     grad_y = cot_all[j].astype(F32) + norm_back(pair_unit, pair_scale, grad_mnorm, merge_gain[...])
     grad_y = dot(pair_of_quarter[...], stacked(grad_y.astype(BF16)), TN).astype(BF16)
     gy_out[...] = grad_y.reshape(4, QUAD, D)
     gy_in[0] = gy_out[3]
     gy_move = roll_in(gy_out, gy_in)
-    so_move = scatter(so_out, so_in)
+
+    arrive(norm_rest)
+    merged = dot(norm_all[...].reshape(lon_size * QUAD, 4 * D), merge_full).astype(BF16)
+    for k in range(KB):
+        part = dot(merged, split_block(k)).astype(BF16)
+        so_out[:, :, MS * k : MS * (k + 1)] = part.reshape(lon_size, QUAD, MS)
+    so_start = reduce_start(so_out, so_mid)
 
     arrive(gy_move)
     grad_rolled_y = gy_in[...].reshape(ROWS, D)
@@ -387,7 +439,11 @@
     few = dot(dense[...], gp[...]).astype(BF16)
     for d in range(lon_size):
         gp_out[d] = few[:, CW * d : CW * (d + 1)]
-    gp_move = scatter(gp_out, gp_in)
+    gp_far = push(gp_out.at[beyond], gp_mid, i, across)
+    gp_move = [
+        push(gp_out.at[across], gp_in.at[j], i, across),
+        push(gp_out.at[mate], gp_in.at[j], i, mate),
+    ]
     gp_in[j] = gp_out[j]
 
     grad_normed = dot(gp[...], inner[...], NT)
@@ -396,7 +452,11 @@
     gf_in[3] = gf_out[0]
     gf_move = roll_out(gf_out, gf_in)
 
-    arrive(toks_move)
+    arrive([gp_far])
+    gp_move.append(push(gp_mid, gp_in.at[across], i, mate))
+    so_crossed = reduce_cross(so_out, so_mid, so_start, 1)
+
+    arrive(toks_rest)
     arrive(gp_move)
     tokens = lon_size * WIN
     summed = dot(toks_all[...].reshape(tokens, D), gp_in[...].reshape(tokens, CW), TN)
@@ -410,13 +470,13 @@
         return dot(to_pair[...], stacked(wide), TN).astype(BF16)
 
     def put(dst, rows):
-        for l in range(LEVELS):
-            for r in range(WIN_LAT):
-                start = (l * WIN_LAT + r) * 16
-                dst[l, r] = rows[start : start + WIN_LON]
-
-    arrive(so_move)
-    put(outputs, from_pairs((y_pairs + total(so_out, so_in)).astype(BF16)))
+        for r in range(WIN_LAT):
+            for c in range(WIN_LON):
+                start = (r * WIN_LON + c) * LEVELS
+                dst[r, c] = rows[start : start + LEVELS]
+
+    split_out = reduce_end(so_out, so_mid, so_crossed, 1)
+    put(outputs, from_pairs((y_pairs + split_out).astype(BF16)))
 
     arrive(dw_move)
     mine = dw_out[y * XH + xh].astype(F32)
@@ -426,7 +486,7 @@
     mine = mine.astype(BF16)
     CB = CW // 3
     tall = jnp.concatenate([mine[:, CB * c : CB * (c + 1)] for c in range(3)], axis=0)
-    row = lax.broadcasted_iota(jnp.int32, (16 * Z, 12 * Z), 0)
+    row = lax.broadcasted_iota(jnp.int32, (16 * Z, 1), 0)
     col = lax.broadcasted_iota(jnp.int32, (16 * Z, 12 * Z), 1)
     inner_row = row % 16
     want = (inner_row // 4) * (4 * Z) + (row // 16) * 4 + inner_row % 4
@@ -460,23 +520,12 @@
 ):
     D = fields.shape[-1]
     to_quarter, to_pair, pair_of_quarter, dense, pick = (jnp.asarray(a) for a in orders())
-    middle = (RELS - 1) // 2
-    wrapped = jnp.concatenate(
-        [
-            bias_table[:, middle::-1],
-            jnp.zeros((HEADS, 2 * SPAN - RELS), F32),
-            bias_table[:, :middle:-1],
-        ],
-        axis=1,
+    vmem = pl.BlockSpec(memory_space=pltpu.VMEM)
+    operands = (
+        fields.transpose(1, 2, 0, 3), to_quarter, split_weight, merge_weight,
+        cotangent.transpose(1, 2, 0, 3), to_pair, norm_gain.reshape(1, D), inner_weight, bias_table,
+        pick, outer_weight, pair_of_quarter, merge_gain.reshape(1, 4 * D), dense,
     )
-    vmem = pl.BlockSpec(memory_space=pltpu.VMEM)
-    bias = pl.pallas_call(
-        bias_kernel,
-        out_shape=jax.ShapeDtypeStruct((HEADS, ROWS, ROWS), F32),
-        in_specs=[vmem] * 2,
-        out_specs=vmem,
-        compiler_params=pltpu.CompilerParams(vmem_limit_bytes=32 * 1024 * 1024),
-    )(wrapped, pick)
     MS, CW = D // 2, 3 * D // lon_size
 
     def buf(*shape, dtype=BF16):
@@ -485,38 +534,43 @@
     quarters = (4, QUAD, D)
     wide = (lon_size, QUAD, 4 * D)
     scratch = [
-        buf(ROWS, D), buf(*quarters), buf(*quarters), buf(*wide), buf(*wide),
-        buf(Z, 16, MS), buf(64, MS, dtype=F32), buf(Y, XH, 8, 2 * Z, MS), buf(Y, Z, XH, 16, MS),
-        buf(*quarters), buf(*quarters), buf(*wide), buf(*wide), buf(*quarters), buf(*quarters),
+        buf(WIN, D), buf(*quarters), buf(*quarters), buf(*wide), buf(*wide),
+        buf(Z, 16, MS), buf(64, MS, dtype=F32), buf(Y, XH, 8, 2 * Z, MS),
+        buf(Y, Z, XH, 16, MS),
+        buf(*quarters), buf(*quarters), buf(*wide), buf(*quarters), buf(*quarters),
         buf(*quarters), buf(*quarters), buf(HEADS, ROWS, ROWS, dtype=F32), buf(ROWS, 3 * D),
         buf(ROWS, D),
         buf(lon_size, WIN, D), buf(ROWS, 3 * D), buf(lon_size, WIN, CW), buf(lon_size, WIN, CW),
         buf(Y * XH, 4 * Z, CW), buf(Y * XH, 4 * Z, CW), buf(Z, 16, CW // 3), buf(Z, 16, CW // 3),
-        buf(*wide), buf(*wide), buf(ROWS, D, dtype=F32),
+        buf(*wide), buf(ROWS, D, dtype=F32), buf(HEADS, ROWS, ROWS, dtype=F32),
+        buf(HEADS, 2 * SPAN, dtype=F32), buf(WIN, CW),
+        buf(2, QUAD, 4 * D), buf(2, QUAD, 4 * D), buf(2, QUAD, 4 * D), buf(2, QUAD, 4 * D),
     ]
-    count = 4 * 3 + 6 * (lon_size - 1) + 2 * 5 + (Y * XH - 1)
+    count = 64
     scratch += [
         pltpu.SemaphoreType.DMA((count,)), pltpu.SemaphoreType.DMA((count,)),
         pltpu.SemaphoreType.DMA((3, Z)), pltpu.SemaphoreType.DMA((3, Z)),
+        pltpu.SemaphoreType.DMA((len(operands),)),
     ]
-    return pl.pallas_call(
+    scratch += [pltpu.VMEM(x.shape, x.dtype) for x in operands]
+    grid_shape = (WIN_LAT, WIN_LON, LEVELS, D)
+    out, grad, sums = pl.pallas_call(
         functools.partial(main_kernel, lon_size),
         out_shape=(
-            jax.ShapeDtypeStruct(fields.shape, BF16),
-            jax.ShapeDtypeStruct(fields.shape, BF16),
+            jax.ShapeDtypeStruct(grid_shape, BF16),
+            jax.ShapeDtypeStruct(grid_shape, BF16),
             jax.ShapeDtypeStruct((4, CW), F32),
         ),
-        in_specs=[vmem] * 13,
+        in_specs=[pl.BlockSpec(memory_space=pltpu.HBM)] * len(operands),
         out_specs=(vmem,) * 3,
         scratch_shapes=scratch,
         compiler_params=pltpu.CompilerParams(
-            collective_id=0, has_side_effects=True, vmem_limit_bytes=48 * 1024 * 1024
+            collective_id=0, has_side_effects=True, vmem_limit_bytes=63 * 1024 * 1024
         ),
     )(
-        fields, cotangent, norm_gain.reshape(1, D), inner_weight, outer_weight, bias,
-        merge_gain.reshape(1, 4 * D), merge_weight, split_weight,
-        to_quarter, to_pair, pair_of_quarter, dense,
+        *operands,
     )
+    return out.transpose(2, 0, 1, 3), grad.transpose(2, 0, 1, 3), sums
 
 
 def solution(mesh):

time: 112 us -> 104 us (0.929)
  Pallas kernels: 103 us -> 98.4 us
  local copies, waits for them, and re-layouts: 7.33 us -> 4.63 us
    pallas_call x1 -> x0, Pallas kernels: 4.17 us -> none  [local(): pl.pallas_call(bias_kernel, out_shape=jax.ShapeDtypeStruct((HEADS, ROWS,...]
    slice x2 -> x0, local copies, waits for them, and re-layouts: 1.63 us -> none  [the longest x1 0.92 us: local(): bias_table[:, :middle:-1]]
    pallas_call x2 -> x0, local copies, waits for them, and re-layouts: 1.63 us -> none  [local(): pl.pallas_call(functools.partial(main_kernel, lon_size), out_shape=(jax.S...]
    unnamed x29 -> x3, local copies, waits for them, and re-layouts: 4 us -> 4.63 us
where the time goes in v2:
time: 104 us
  Pallas kernels  98.4 us (95%)
  local copies, waits for them, and re-layouts  4.63 us (4%)
    pallas_call x1, Pallas kernels, local(): pl.pallas_call(functools.partial(main_kernel, lon_size), out_shape=(jax.S...  98.4 us
    unnamed x3, local copies, waits for them, and re-layouts  4.63 us

profile of v2, /device:TPU:1, one launch (start us, length us, event | category | flops | bytes accessed | tf_op | source)
XLA Modules:
  0.0 103.6 jit_solution(715363710536575994)
XLA Ops:
  0.6 98.4 %shard_map.157 = (bf16[6,12,2,512]{3,2,1,0:T(2,128)(2,1)}, bf16[6,12,2,512]{3,2,1,0:T(2,128)(2,1)}, f32[4,384]{1,0:T(4,128)}) custom-call(bf16[6,12,2,512]{3,2,1,0:T(2,128)(2,1)} %bitcast.6, bf16[192,144]{1,0:T(8,128)(2,1)} %constant.10.clone.refs_1_, bf16[8,2048]{1,0:T(8,128)(2,1)} %refs_2_.1, bf16[16,1024]{1,0:T(8,128)(2,1)} %refs_3_.1, ...), custom_call_target="tpu_custom_call" | custom-call | tf_op jit(solution)/shard_map/pallas_call | solution.py:557
  99.0 1.7 %copy.20 = bf16[2,6,12,512]{3,0,2,1:T(2,128)(2,1)} copy(bf16[2,6,12,512]{3,0,2,1:T(2,128)(2,1)} %bitcast.9) | data formatting | bytes 294912
  100.7 1.7 %copy.21 = bf16[2,6,12,512]{3,0,2,1:T(2,128)(2,1)} copy(bf16[2,6,12,512]{3,0,2,1:T(2,128)(2,1)} %bitcast.8) | data formatting | bytes 294912
  102.3 1.3 %copy.22 = f32[4,384]{1,0:T(4,128)} copy(f32[4,384]{1,0:T(4,128)} %get-tuple-element.14) | data formatting | bytes 12288

commit v3 on v2

--- a/solution.py
+++ b/solution.py
@@ -21,6 +21,9 @@
 WIN = 144
 FAR = -1e30
 Y, Z, XH = 4, 16, 2
+FIRST = (6, -6, 3, -3, 8, 1, -1)
+Z_FAR_FIRST = sorted(range(1, Z), key=lambda d: -min(d, Z - d))
+SECOND = ((-1, 1), (1, -1), (-3, 1), (3, -1), (6, 1), (-6, -1), (-6, 1), (6, -1))
 MESH = pl.DeviceIdType.MESH
 NT = (((1,), (1,)), ((), ()))
 TN = (((0,), (0,)), ((), ()))
@@ -115,7 +118,7 @@
     for load in loads:
         load.start()
     (
-        fields, to_quarter, split_shard, merge_shard, cotangent, to_pair, gain, inner, table,
+        split_shard, merge_shard, fields, to_quarter, cotangent, to_pair, gain, inner, table,
         pick, outer, pair_of_quarter, merge_gain, dense,
     ) = local_refs
     loads = dict(zip(map(id, local_refs), loads))
@@ -180,25 +183,9 @@
     for dy, dx in plane:
         partners.append((at(y_by(dy), z, lax.rem(xh + dx, XH)), j))
     barrier = pltpu.get_barrier_semaphore()
+    partners = [(at(y, z_by(d), xh), j) for d in Z_FAR_FIRST] + partners
     for lat, lon in partners:
         pl.semaphore_signal(barrier, inc=1, device_id=(lat, lon), device_id_type=MESH)
-
-    @pl.loop(1, Z)
-    def _(d):
-        pl.semaphore_signal(
-            barrier, inc=1, device_id=(at(y, z_by(d), xh), j), device_id_type=MESH
-        )
-
-    def to_natural(src):
-        for r in range(WIN_LAT):
-            for c in range(WIN_LON):
-                start = (r * WIN_LON + c) * LEVELS
-                nat[start : start + LEVELS, :] = src[r, c]
-        return nat[...]
-
-    ready(fields, to_quarter)
-    quads[...] = dot(to_quarter[...], to_natural(fields)).astype(BF16).reshape(4, QUAD, D)
-    win[0] = quads[3]
 
     ready(split_shard, merge_shard)
     for k in range(KB):
@@ -213,7 +200,7 @@
     sel = (col == 8 * place + 2 * j + own % 2).astype(F32).astype(BF16)
     merge_w[y, z, xh] = dot(merge_shard[...], sel).astype(BF16)
 
-    pl.semaphore_wait(barrier, len(partners) + Z - 1)
+    pl.semaphore_wait(barrier, len(partners))
 
     def roll_in(src, dst):
         return [
@@ -227,35 +214,63 @@
             for a, b in ((0, 1), (1, 0), (1, 1))
         ]
 
-    def z_copy(kind, d, src, dst):
+    def z_send(kind, slot, r, d):
+        block, k = slot(z_by(r)), (r - d) % Z
+        pltpu.make_async_remote_copy(
+            src_ref=block, dst_ref=block, send_sem=zsend.at[kind, k], recv_sem=zrecv.at[kind, k],
+            device_id=(at(y, z_by(d % Z), xh), j), device_id_type=MESH,
+        ).start()
+
+    def z_wait(kind, slot, steps, received=True):
+        for e in steps:
+            block, k = slot(z_by(e % Z)), e % Z
+            copy = pltpu.make_async_remote_copy(
+                src_ref=block, dst_ref=block, send_sem=zsend.at[kind, k], recv_sem=zrecv.at[kind, k],
+                device_id=(at(y, z_by(1), xh), j), device_id_type=MESH,
+            )
+            if received:
+                copy.wait_recv()
+            else:
+                copy.wait_send()
+
+    def raw_slot(k):
+        return raw.at[k]
+
+    def merge_slot(k):
+        return merge_w.at[y, k, xh]
+
+    def z_first(kind, slot):
+        for d in FIRST:
+            z_send(kind, slot, 0, d)
+
+    def z_second(kind, slot):
+        z_wait(kind, slot, [-d for d in FIRST if abs(d) < Z // 2])
+        for r, d in SECOND:
+            z_send(kind, slot, r % Z, d)
+
+    def z_third(kind, slot):
+        z_wait(kind, slot, [e for e in range(1, Z) if e not in [-d % Z for d in FIRST if abs(d) < Z // 2]])
+
+    def sums_z(d):
         return pltpu.make_async_remote_copy(
-            src_ref=src, dst_ref=dst, send_sem=zsend.at[kind, d], recv_sem=zrecv.at[kind, d],
+            src_ref=z_out.at[z_by(d)], dst_ref=z_in.at[z], send_sem=zsend.at[2, d], recv_sem=zrecv.at[2, d],
             device_id=(at(y, z_by(d), xh), j), device_id_type=MESH,
         )
 
-    def split_z(d):
-        return z_copy(0, d, raw.at[z], raw.at[z])
-
-    def merge_z(d):
-        return z_copy(1, d, merge_w.at[y, z, xh], merge_w.at[y, z, xh])
-
-    def sums_z(d):
-        return z_copy(2, d, z_out.at[z_by(d)], z_in.at[z])
-
-    def z_start(make):
-        @pl.loop(1, Z)
-        def _(d):
-            make(d).start()
-
-    def z_arrive(make):
-        @pl.loop(1, Z)
-        def _(d):
-            make(d).wait_recv()
-
+    z_first(0, raw_slot)
+    z_first(1, merge_slot)
+
+    def to_natural(src):
+        for r in range(WIN_LAT):
+            for c in range(WIN_LON):
+                start = (r * WIN_LON + c) * LEVELS
+                nat[start : start + LEVELS, :] = src[r, c]
+        return nat[...]
+
+    ready(fields, to_quarter)
+    quads[...] = dot(to_quarter[...], to_natural(fields)).astype(BF16).reshape(4, QUAD, D)
+    win[0] = quads[3]
     fields_move = roll_in(quads, win)
-
-    z_start(split_z)
-    z_start(merge_z)
 
     def gather_start(whole):
         mine = whole.at[j]
@@ -287,6 +302,10 @@
     ready(cotangent, to_pair)
     cot_all[j] = lanes(dot(to_pair[...], to_natural(cotangent)).astype(BF16))
 
+    ready(table, pick)
+    make_bias(table, padded, pick[...], bias)
+    z_second(0, raw_slot)
+    z_second(1, merge_slot)
     arrive(fields_move)
     rolled = win[...].reshape(ROWS, D).astype(F32)
     ready(gain, inner)
@@ -295,18 +314,15 @@
     normed[...] = (unit * gain[...]).astype(BF16)
     proj[...] = dot(normed[...], inner[...]).astype(BF16)
 
-    ready(table, pick)
-    make_bias(table, padded, pick[...], bias)
-
     full = Z * 16
     out = lax.broadcasted_iota(jnp.int32, (full, 1), 0)
     src = lax.broadcasted_iota(jnp.int32, (full, full), 1)
     want = ((out % (2 * Z)) // 2) * 16 + (out // (2 * Z)) * 2 + out % 2
     regroup = (src == want).astype(F32).astype(BF16)
-    z_arrive(split_z)
+    z_third(0, raw_slot)
     split_w[y, xh] = dot(regroup, raw[...].reshape(full, MS)).astype(BF16).reshape(KB, 2 * Z, MS)
     split_x = push(split_w.at[y, xh], split_w.at[y, xh], at(y, z, other), j)
-    z_arrive(merge_z)
+    z_third(1, merge_slot)
     merge_x = push(merge_w.at[y, :, xh], merge_w.at[y, :, xh], at(y, z, other), j)
 
     def y_spread(whole):
@@ -314,7 +330,6 @@
 
     arrive([split_x])
     split_y = y_spread(split_w)
-    cot_move = gather_start(cot_all)
 
     half_q = lax.broadcasted_iota(jnp.int32, (ROWS, 1), 0) // (2 * QUAD)
     half_k = lax.broadcasted_iota(jnp.int32, (1, ROWS), 1) // (2 * QUAD)
@@ -344,6 +359,15 @@
 
     arrive([merge_x])
     merge_y = y_spread(merge_w)
+    cot_move = gather_start(cot_all)
+
+    attended += [attend(2), attend(3)]
+    attended = jnp.concatenate(attended, axis=1)
+    ready(outer)
+    y_rolled = (rolled + dot(attended, outer[...])).astype(BF16)
+    y_out[...] = y_rolled.reshape(4, QUAD, D)
+    y_in[3] = y_out[0]
+    y_move = roll_out(y_out, y_in)
 
     row = lax.broadcasted_iota(jnp.int32, (D, D), 0)
     col = lax.broadcasted_iota(jnp.int32, (1, D), 1)
@@ -353,15 +377,7 @@
     ready(dense)
     toks = dot(dense[...], normed[...]).astype(BF16)
     toks_all[j] = dot(toks, swap).astype(BF16)
-    toks_move = gather_start(toks_all)
-
-    attended += [attend(2), attend(3)]
-    attended = jnp.concatenate(attended, axis=1)
-    ready(outer)
-    y_rolled = (rolled + dot(attended, outer[...])).astype(BF16)
-    y_out[...] = y_rolled.reshape(4, QUAD, D)
-    y_in[3] = y_out[0]
-    y_move = roll_out(y_out, y_in)
+
 
     def y_forward(whole, halves):
         return [
@@ -379,6 +395,7 @@
     pair_unit, pair_scale = norm_parts(y_pairs)
     norm_all[j] = (pair_unit * merge_gain[...]).astype(BF16)
     norm_move = gather_start(norm_all)
+    toks_move = gather_start(toks_all)
 
     arrive(merge_y)
     merge_f = y_forward(merge_w, lambda w, yy, part: w.at[yy, pl.ds(part * (Z // 2), Z // 2)])
@@ -418,6 +435,7 @@
     so_start = reduce_start(so_out, so_mid)
 
     arrive(gy_move)
+    so_crossed = reduce_cross(so_out, so_mid, so_start, 1)
     grad_rolled_y = gy_in[...].reshape(ROWS, D)
     grad_attended = dot(grad_rolled_y, outer[...], NT).astype(BF16)
     for pair in range(HEADS // 2):
@@ -454,12 +472,13 @@
 
     arrive([gp_far])
     gp_move.append(push(gp_mid, gp_in.at[across], i, mate))
-    so_crossed = reduce_cross(so_out, so_mid, so_start, 1)
 
     arrive(toks_rest)
-    arrive(gp_move)
-    tokens = lon_size * WIN
-    summed = dot(toks_all[...].reshape(tokens, D), gp_in[...].reshape(tokens, CW), TN)
+    arrive(gp_move[:2])
+    summed = dot(toks_all[j], gp_in[j], TN) + dot(toks_all[mate], gp_in[mate], TN)
+    summed = summed + dot(toks_all[across], gp_in[across], TN)
+    arrive(gp_move[2:])
+    summed = summed + dot(toks_all[beyond], gp_in[beyond], TN)
     dw_out[...] = summed.astype(BF16).reshape(Y * XH, 4 * Z, CW)
     dw_move = []
     for dy, dx in plane:
@@ -474,9 +493,6 @@
             for c in range(WIN_LON):
                 start = (r * WIN_LON + c) * LEVELS
                 dst[r, c] = rows[start : start + LEVELS]
-
-    split_out = reduce_end(so_out, so_mid, so_crossed, 1)
-    put(outputs, from_pairs((y_pairs + split_out).astype(BF16)))
 
     arrive(dw_move)
     mine = dw_out[y * XH + xh].astype(F32)
@@ -492,13 +508,21 @@
     want = (inner_row // 4) * (4 * Z) + (row // 16) * 4 + inner_row % 4
     spread = jnp.logical_and(col == want, inner_row < 12).astype(F32).astype(BF16)
     z_out[...] = dot(spread, tall).astype(BF16).reshape(Z, 16, CB)
-    z_start(sums_z)
+
+    for d in Z_FAR_FIRST:
+        sums_z(d).start()
     z_in[z] = z_out[z]
+
+    split_out = reduce_end(so_out, so_mid, so_crossed, 1)
+    put(outputs, from_pairs((y_pairs + split_out).astype(BF16)))
 
     arrive(gf_move)
     put(grad_fields, dot(to_quarter[...], gf_in[...].reshape(ROWS, D), TN).astype(BF16))
 
-    z_arrive(sums_z)
+    @pl.loop(1, Z)
+    def _(d):
+        sums_z(d).wait_recv()
+
     owned = jnp.sum(z_in[...].astype(F32), axis=0)
     shrink = 1.0 / math.sqrt(WIN * lat_size * lon_size)
     for c in range(3):
@@ -509,9 +533,23 @@
 
     @pl.loop(1, Z)
     def _(d):
-        split_z(d).wait_send()
-        merge_z(d).wait_send()
         sums_z(d).wait_send()
+
+    for kind, slot in enumerate((raw_slot, merge_slot)):
+        z_wait(kind, slot, range(1, Z), received=False)
+
+
+def settle_kernel(*refs):
+    sources, targets, held, sems = refs[:3], refs[3:6], refs[6:9], refs[9]
+    loads = [pltpu.make_async_copy(a, b, sems.at[0, k]) for k, (a, b) in enumerate(zip(sources, held))]
+    stores = [pltpu.make_async_copy(a, b, sems.at[1, k]) for k, (a, b) in enumerate(zip(held, targets))]
+    for load in loads:
+        load.start()
+    for load, store in zip(loads, stores):
+        load.wait()
+        store.start()
+    for store in stores:
+        store.wait()
 
 
 def local(
@@ -522,7 +560,7 @@
     to_quarter, to_pair, pair_of_quarter, dense, pick = (jnp.asarray(a) for a in orders())
     vmem = pl.BlockSpec(memory_space=pltpu.VMEM)
     operands = (
-        fields.transpose(1, 2, 0, 3), to_quarter, split_weight, merge_weight,
+        split_weight, merge_weight, fields.transpose(1, 2, 0, 3), to_quarter,
         cotangent.transpose(1, 2, 0, 3), to_pair, norm_gain.reshape(1, D), inner_weight, bias_table,
         pick, outer_weight, pair_of_quarter, merge_gain.reshape(1, 4 * D), dense,
     )
@@ -570,6 +608,19 @@
     )(
         *operands,
     )
+    results = (out, grad, sums)
+    hbm = pl.BlockSpec(memory_space=pltpu.HBM)
+    out, grad, sums = pl.pallas_call(
+        settle_kernel,
+        out_shape=tuple(jax.ShapeDtypeStruct(x.shape, x.dtype) for x in results),
+        in_specs=[hbm] * 3,
+        out_specs=(hbm,) * 3,
+        scratch_shapes=[
+            *(pltpu.VMEM(x.shape, x.dtype) for x in results),
+            pltpu.SemaphoreType.DMA((2, 3)),
+        ],
+        compiler_params=pltpu.CompilerParams(vmem_limit_bytes=63 * 1024 * 1024),
+    )(*results)
     return out.transpose(2, 0, 1, 3), grad.transpose(2, 0, 1, 3), sums
 
 

time: 104 us -> 97.7 us (0.939)
  local copies, waits for them, and re-layouts: 4.63 us -> 0 us
  Pallas kernels: 98.4 us -> 96.4 us
    unnamed x3 -> x0, local copies, waits for them, and re-layouts: 4.63 us -> none
    pallas_call x1, Pallas kernels: 98.4 us -> 94.7 us  [local(): pl.pallas_call(functools.partial(main_kernel, lon_size), out_shape=(jax.S...]
    pallas_call x0 -> x1, Pallas kernels: none -> 1.7 us  [local(): pl.pallas_call(settle_kernel, out_shape=tuple((jax.ShapeDtypeStruct(x.sha...]
where the time goes in v3:
time: 97.7 us; the launch traced here: 97 us
  Pallas kernels  96.4 us (99%)
    pallas_call x1, Pallas kernels, local(): pl.pallas_call(functools.partial(main_kernel, lon_size), out_shape=(jax.S...  94.7 us

profile of v3, /device:TPU:1, one launch (start us, length us, event | category | flops | bytes accessed | tf_op | source)
XLA Modules:
  0.0 97.0 jit_solution(15825183989625881293)
XLA Ops:
  0.6 94.7 %shard_map.157 = (bf16[6,12,2,512]{3,2,1,0:T(2,128)(2,1)}, bf16[6,12,2,512]{3,2,1,0:T(2,128)(2,1)}, f32[4,384]{1,0:T(4,128)}) custom-call(bf16[8,2048]{1,0:T(8,128)(2,1)} %refs_0_.1, bf16[16,1024]{1,0:T(8,128)(2,1)} %refs_1_.1, bf16[6,12,2,512]{3,2,1,0:T(2,128)(2,1)} %bitcast.6, bf16[192,144]{1,0:T(8,128)(2,1)} %constant.10.clone.refs_3_, ...), custom_call_target="tpu_custom_call" | custom-call | tf_op jit(solution)/shard_map/pallas_call | solution.py:595
  95.3 1.7 %shard_map.158 = (bf16[6,12,2,512]{3,2,1,0:T(2,128)(2,1)}, bf16[6,12,2,512]{3,2,1,0:T(2,128)(2,1)}, f32[4,384]{1,0:T(4,128)}) custom-call(bf16[6,12,2,512]{3,2,1,0:T(2,128)(2,1)} %get-tuple-element.9.refs_0_, bf16[6,12,2,512]{3,2,1,0:T(2,128)(2,1)} %get-tuple-element.10.refs_1_, f32[4,384]{1,0:T(4,128)} %get-tuple-element.11.refs_2_), custom_call_target="tpu_custom_call" | custom-call | tf_op jit(solution)/shard_map/pallas_call | solution.py:613

commit v4 on v3

--- a/solution.py
+++ b/solution.py
@@ -103,12 +103,12 @@
 ):
     operands, refs = refs[:14], refs[14:]
     (
-        outputs, grad_fields, grad_inner,
+        outputs_hbm, grad_fields_hbm, grad_inner,
         nat, quads, win, cot_all, norm_all, raw, stack, split_w, merge_w,
         y_out, y_in, gm_out, gy_out, gy_in, gf_out, gf_in, att, proj, normed,
         toks_all, gp, gp_out, gp_in, dw_out, dw_in, z_out, z_in, so_out, unit_keep,
         bias, padded, gp_mid, gm_mid, so_mid, cross_out, cross_in,
-        ssem, rsem, zsend, zrecv, lsem,
+        ssem, rsem, zsend, zrecv, lsem, outputs, grad_fields, osem,
         *local_refs,
     ) = refs
     loads = [
@@ -205,13 +205,13 @@
     def roll_in(src, dst):
         return [
             push(src.at[(1 - a) * 2 + 1 - b], dst.at[a * 2 + b], lat_by(-a), lon_by(-b))
-            for a, b in ((0, 1), (1, 0), (1, 1))
+            for a, b in ((1, 1), (1, 0), (0, 1))
         ]
 
     def roll_out(src, dst):
         return [
             push(src.at[a * 2 + b], dst.at[(1 - a) * 2 + 1 - b], lat_by(a), lon_by(b))
-            for a, b in ((0, 1), (1, 0), (1, 1))
+            for a, b in ((1, 1), (1, 0), (0, 1))
         ]
 
     def z_send(kind, slot, r, d):
@@ -282,12 +282,12 @@
         return started[1], push(came, came, i, mate)
 
     def reduce_start(src, mid):
-        return push(src.at[mate], mid.at[0], i, mate), push(src.at[beyond], mid.at[1], i, mate)
+        return push(src.at[beyond], mid.at[1], i, mate), push(src.at[mate], mid.at[0], i, mate)
 
     def reduce_cross(src, mid, started, slot):
-        arrive(started)
+        arrive(started[:1])
         cross_out[slot] = (src[across].astype(F32) + mid[1].astype(F32)).astype(BF16)
-        return [push(cross_out.at[slot], cross_in.at[slot], i, across)]
+        return [started[1], push(cross_out.at[slot], cross_in.at[slot], i, across)]
 
     def reduce_end(src, mid, crossed, slot):
         arrive(crossed)
@@ -481,7 +481,7 @@
     summed = summed + dot(toks_all[beyond], gp_in[beyond], TN)
     dw_out[...] = summed.astype(BF16).reshape(Y * XH, 4 * Z, CW)
     dw_move = []
-    for dy, dx in plane:
+    for dy, dx in sorted(plane, key=lambda p: -min(p[0], Y - p[0]) - 2 * p[1]):
         yy, xx = y_by(dy), lax.rem(xh + dx, XH)
         dw_move.append(push(dw_out.at[yy * XH + xx], dw_in.at[y * XH + xh], at(yy, z, xx), j))
 
@@ -515,9 +515,13 @@
 
     split_out = reduce_end(so_out, so_mid, so_crossed, 1)
     put(outputs, from_pairs((y_pairs + split_out).astype(BF16)))
+    stores = [pltpu.make_async_copy(outputs, outputs_hbm, osem.at[0])]
+    stores[0].start()
 
     arrive(gf_move)
     put(grad_fields, dot(to_quarter[...], gf_in[...].reshape(ROWS, D), TN).astype(BF16))
+    stores.append(pltpu.make_async_copy(grad_fields, grad_fields_hbm, osem.at[1]))
+    stores[1].start()
 
     @pl.loop(1, Z)
     def _(d):
@@ -528,6 +532,8 @@
     for c in range(3):
         grad_inner[:, CB * c : CB * (c + 1)] = owned[4 * c : 4 * c + 4] * shrink
 
+    for store in stores:
+        store.wait()
     for copy in sent:
         copy.wait_send()
 
@@ -559,6 +565,7 @@
     D = fields.shape[-1]
     to_quarter, to_pair, pair_of_quarter, dense, pick = (jnp.asarray(a) for a in orders())
     vmem = pl.BlockSpec(memory_space=pltpu.VMEM)
+    hbm = pl.BlockSpec(memory_space=pltpu.HBM)
     operands = (
         split_weight, merge_weight, fields.transpose(1, 2, 0, 3), to_quarter,
         cotangent.transpose(1, 2, 0, 3), to_pair, norm_gain.reshape(1, D), inner_weight, bias_table,
@@ -589,6 +596,8 @@
         pltpu.SemaphoreType.DMA((count,)), pltpu.SemaphoreType.DMA((count,)),
         pltpu.SemaphoreType.DMA((3, Z)), pltpu.SemaphoreType.DMA((3, Z)),
         pltpu.SemaphoreType.DMA((len(operands),)),
+        buf(WIN_LAT, WIN_LON, LEVELS, D), buf(WIN_LAT, WIN_LON, LEVELS, D),
+        pltpu.SemaphoreType.DMA((2,)),
     ]
     scratch += [pltpu.VMEM(x.shape, x.dtype) for x in operands]
     grid_shape = (WIN_LAT, WIN_LON, LEVELS, D)
@@ -599,8 +608,8 @@
             jax.ShapeDtypeStruct(grid_shape, BF16),
             jax.ShapeDtypeStruct((4, CW), F32),
         ),
-        in_specs=[pl.BlockSpec(memory_space=pltpu.HBM)] * len(operands),
-        out_specs=(vmem,) * 3,
+        in_specs=[hbm] * len(operands),
+        out_specs=(hbm, hbm, vmem),
         scratch_shapes=scratch,
         compiler_params=pltpu.CompilerParams(
             collective_id=0, has_side_effects=True, vmem_limit_bytes=63 * 1024 * 1024
@@ -609,7 +618,6 @@
         *operands,
     )
     results = (out, grad, sums)
-    hbm = pl.BlockSpec(memory_space=pltpu.HBM)
     out, grad, sums = pl.pallas_call(
         settle_kernel,
         out_shape=tuple(jax.ShapeDtypeStruct(x.shape, x.dtype) for x in results),

time: 97.7 us -> 95.8 us (0.981)
  Pallas kernels: 96.4 us -> 93.9 us
    pallas_call x1, Pallas kernels: 94.7 us -> 92.2 us  [local(): pl.pallas_call(functools.partial(main_kernel, lon_size), out_shape=(jax.S...]
where the time goes in v4:
time: 95.8 us; the launch traced here: 94.6 us
  Pallas kernels  93.9 us (98%)
    pallas_call x1, Pallas kernels, local(): pl.pallas_call(functools.partial(main_kernel, lon_size), out_shape=(jax.S...  92.2 us

profile of v4, /device:TPU:1, one launch (start us, length us, event | category | flops | bytes accessed | tf_op | source)
XLA Modules:
  0.0 94.6 jit_solution(1675831556962736040)
XLA Ops:
  0.6 92.2 %shard_map.157 = (bf16[6,12,2,512]{3,2,1,0:T(2,128)(2,1)}, bf16[6,12,2,512]{3,2,1,0:T(2,128)(2,1)}, f32[4,384]{1,0:T(4,128)}) custom-call(bf16[8,2048]{1,0:T(8,128)(2,1)} %refs_0_.1, bf16[16,1024]{1,0:T(8,128)(2,1)} %refs_1_.1, bf16[6,12,2,512]{3,2,1,0:T(2,128)(2,1)} %bitcast.6, bf16[192,144]{1,0:T(8,128)(2,1)} %constant.10.clone.refs_3_, ...), custom_call_target="tpu_custom_call" | custom-call | tf_op jit(solution)/shard_map/pallas_call | solution.py:604
  92.9 1.7 %shard_map.158 = (bf16[6,12,2,512]{3,2,1,0:T(2,128)(2,1)}, bf16[6,12,2,512]{3,2,1,0:T(2,128)(2,1)}, f32[4,384]{1,0:T(4,128)}) custom-call(bf16[6,12,2,512]{3,2,1,0:T(2,128)(2,1)} %get-tuple-element.9.refs_0_, bf16[6,12,2,512]{3,2,1,0:T(2,128)(2,1)} %get-tuple-element.10.refs_1_, f32[4,384]{1,0:T(4,128)} %get-tuple-element.11.refs_2_), custom_call_target="tpu_custom_call" | custom-call | tf_op jit(solution)/shard_map/pallas_call | solution.py:621

commit v5 on v4

--- a/solution.py
+++ b/solution.py
@@ -107,7 +107,7 @@
         nat, quads, win, cot_all, norm_all, raw, stack, split_w, merge_w,
         y_out, y_in, gm_out, gy_out, gy_in, gf_out, gf_in, att, proj, normed,
         toks_all, gp, gp_out, gp_in, dw_out, dw_in, z_out, z_in, so_out, unit_keep,
-        bias, padded, gp_mid, gm_mid, so_mid, cross_out, cross_in,
+        bias, padded, gp_mid, gm_mid, gm_far_out, gm_far_in, gm_sum, so_mid, cross_out, cross_in,
         ssem, rsem, zsend, zrecv, lsem, outputs, grad_fields, osem,
         *local_refs,
     ) = refs
@@ -411,16 +411,32 @@
     for k in range(1, KB):
         grad_merged = grad_merged + dot(cots[:, MS * k : MS * (k + 1)], split_block(k), NT)
     grad_merged = grad_merged.astype(BF16)
+    near = (0, 1, -1, 2)
+
+    def gm_part(first, count):
+        for k in range(first, first + count):
+            block = merge_w[y_by(near[k])].reshape(D, MS)
+            gm_out[:, k] = dot(grad_merged, block, NT).astype(BF16).reshape(lon_size, QUAD, D)
+        part = pl.ds(first, count)
+        there = push(gm_out.at[beyond, part], gm_mid.at[1, part], i, mate)
+        here = push(gm_out.at[mate, part], gm_mid.at[0, part], i, mate)
+        arrive([there])
+        pair = gm_out[across, part].astype(F32) + gm_mid[1, part].astype(F32)
+        gm_far_out[part] = pair.astype(BF16)
+        return [here, push(gm_far_out.at[part], gm_far_in.at[part], i, across)]
+
+    gm_moves = gm_part(0, 3)
     arrive(merge_f)
+    gm_moves += gm_part(3, 1)
     merge_full = merge_w[...].reshape(4 * D, MS)
-    gm_out[...] = dot(grad_merged, merge_full, NT).astype(BF16).reshape(lon_size, QUAD, 4 * D)
-
-    gm_start = reduce_start(gm_out, gm_mid)
-    gm_crossed = reduce_cross(gm_out, gm_mid, gm_start, 0)
     norm_rest = gather_relay(norm_all, norm_move)
     toks_rest = gather_relay(toks_all, toks_move)
 
-    grad_mnorm = reduce_end(gm_out, gm_mid, gm_crossed, 0)
+    arrive(gm_moves)
+    for k in range(4):
+        found = gm_out[j, k].astype(F32) + gm_mid[0, k].astype(F32) + gm_far_in[k].astype(F32)
+        gm_sum[y_by(near[k])] = found
+    grad_mnorm = jnp.concatenate([gm_sum[k] for k in range(4)], axis=1)
     grad_y = cot_all[j].astype(F32) + norm_back(pair_unit, pair_scale, grad_mnorm, merge_gain[...])
     grad_y = dot(pair_of_quarter[...], stacked(grad_y.astype(BF16)), TN).astype(BF16)
     gy_out[...] = grad_y.reshape(4, QUAD, D)
@@ -582,14 +598,15 @@
         buf(WIN, D), buf(*quarters), buf(*quarters), buf(*wide), buf(*wide),
         buf(Z, 16, MS), buf(64, MS, dtype=F32), buf(Y, XH, 8, 2 * Z, MS),
         buf(Y, Z, XH, 16, MS),
-        buf(*quarters), buf(*quarters), buf(*wide), buf(*quarters), buf(*quarters),
+        buf(*quarters), buf(*quarters), buf(lon_size, 4, QUAD, D), buf(*quarters), buf(*quarters),
         buf(*quarters), buf(*quarters), buf(HEADS, ROWS, ROWS, dtype=F32), buf(ROWS, 3 * D),
         buf(ROWS, D),
         buf(lon_size, WIN, D), buf(ROWS, 3 * D), buf(lon_size, WIN, CW), buf(lon_size, WIN, CW),
         buf(Y * XH, 4 * Z, CW), buf(Y * XH, 4 * Z, CW), buf(Z, 16, CW // 3), buf(Z, 16, CW // 3),
         buf(*wide), buf(ROWS, D, dtype=F32), buf(HEADS, ROWS, ROWS, dtype=F32),
         buf(HEADS, 2 * SPAN, dtype=F32), buf(WIN, CW),
-        buf(2, QUAD, 4 * D), buf(2, QUAD, 4 * D), buf(2, QUAD, 4 * D), buf(2, QUAD, 4 * D),
+        buf(2, 4, QUAD, D), buf(4, QUAD, D), buf(4, QUAD, D), buf(4, QUAD, D, dtype=F32),
+        buf(2, QUAD, 4 * D), buf(2, QUAD, 4 * D), buf(2, QUAD, 4 * D),
     ]
     count = 64
     scratch += [

time: 95.8 us -> 94.1 us (0.982)
  Pallas kernels: 93.9 us -> 92.2 us
    pallas_call x1, Pallas kernels: 92.2 us -> 90.5 us  [local(): pl.pallas_call(functools.partial(main_kernel, lon_size), out_shape=(jax.S...]
where the time goes in v5:
time: 94.1 us; the launch traced here: 92.8 us
  Pallas kernels  92.2 us (98%)
    pallas_call x1, Pallas kernels, local(): pl.pallas_call(functools.partial(main_kernel, lon_size), out_shape=(jax.S...  90.5 us

profile of v5, /device:TPU:1, one launch (start us, length us, event | category | flops | bytes accessed | tf_op | source)
XLA Modules:
  0.0 92.8 jit_solution(2468100131723711451)
XLA Ops:
  0.6 90.5 %shard_map.157 = (bf16[6,12,2,512]{3,2,1,0:T(2,128)(2,1)}, bf16[6,12,2,512]{3,2,1,0:T(2,128)(2,1)}, f32[4,384]{1,0:T(4,128)}) custom-call(bf16[8,2048]{1,0:T(8,128)(2,1)} %refs_0_.1, bf16[16,1024]{1,0:T(8,128)(2,1)} %refs_1_.1, bf16[6,12,2,512]{3,2,1,0:T(2,128)(2,1)} %bitcast.6, bf16[192,144]{1,0:T(8,128)(2,1)} %constant.10.clone.refs_3_, ...), custom_call_target="tpu_custom_call" | custom-call | tf_op jit(solution)/shard_map/pallas_call | solution.py:621
  91.1 1.7 %shard_map.158 = (bf16[6,12,2,512]{3,2,1,0:T(2,128)(2,1)}, bf16[6,12,2,512]{3,2,1,0:T(2,128)(2,1)}, f32[4,384]{1,0:T(4,128)}) custom-call(bf16[6,12,2,512]{3,2,1,0:T(2,128)(2,1)} %get-tuple-element.9.refs_0_, bf16[6,12,2,512]{3,2,1,0:T(2,128)(2,1)} %get-tuple-element.10.refs_1_, f32[4,384]{1,0:T(4,128)} %get-tuple-element.11.refs_2_), custom_call_target="tpu_custom_call" | custom-call | tf_op jit(solution)/shard_map/pallas_call | solution.py:638

commit v6 on v5

--- a/solution.py
+++ b/solution.py
@@ -450,8 +450,8 @@
         so_out[:, :, MS * k : MS * (k + 1)] = part.reshape(lon_size, QUAD, MS)
     so_start = reduce_start(so_out, so_mid)
 
+    so_crossed = reduce_cross(so_out, so_mid, so_start, 1)
     arrive(gy_move)
-    so_crossed = reduce_cross(so_out, so_mid, so_start, 1)
     grad_rolled_y = gy_in[...].reshape(ROWS, D)
     grad_attended = dot(grad_rolled_y, outer[...], NT).astype(BF16)
     for pair in range(HEADS // 2):

time: 94.1 us -> 91.7 us (0.974)
  Pallas kernels: 92.2 us -> 90.3 us
    pallas_call x1, Pallas kernels: 90.5 us -> 88.6 us  [local(): pl.pallas_call(functools.partial(main_kernel, lon_size), out_shape=(jax.S...]
where the time goes in v6:
time: 91.7 us; the launch traced here: 91 us
  Pallas kernels  90.3 us (98%)
    pallas_call x1, Pallas kernels, local(): pl.pallas_call(functools.partial(main_kernel, lon_size), out_shape=(jax.S...  88.6 us

profile of v6, /device:TPU:1, one launch (start us, length us, event | category | flops | bytes accessed | tf_op | source)
XLA Modules:
  0.0 91.0 jit_solution(6250973727445466779)
XLA Ops:
  0.6 88.6 %shard_map.157 = (bf16[6,12,2,512]{3,2,1,0:T(2,128)(2,1)}, bf16[6,12,2,512]{3,2,1,0:T(2,128)(2,1)}, f32[4,384]{1,0:T(4,128)}) custom-call(bf16[8,2048]{1,0:T(8,128)(2,1)} %refs_0_.1, bf16[16,1024]{1,0:T(8,128)(2,1)} %refs_1_.1, bf16[6,12,2,512]{3,2,1,0:T(2,128)(2,1)} %bitcast.6, bf16[192,144]{1,0:T(8,128)(2,1)} %constant.10.clone.refs_3_, ...), custom_call_target="tpu_custom_call" | custom-call | tf_op jit(solution)/shard_map/pallas_call | solution.py:621
  89.3 1.7 %shard_map.158 = (bf16[6,12,2,512]{3,2,1,0:T(2,128)(2,1)}, bf16[6,12,2,512]{3,2,1,0:T(2,128)(2,1)}, f32[4,384]{1,0:T(4,128)}) custom-call(bf16[6,12,2,512]{3,2,1,0:T(2,128)(2,1)} %get-tuple-element.9.refs_0_, bf16[6,12,2,512]{3,2,1,0:T(2,128)(2,1)} %get-tuple-element.10.refs_1_, f32[4,384]{1,0:T(4,128)} %get-tuple-element.11.refs_2_), custom_call_target="tpu_custom_call" | custom-call | tf_op jit(solution)/shard_map/pallas_call | solution.py:638
